TPU v7x, 256 devices: a whole 4x4x8 slice. The times are simulated.
256 devices in a mesh: gz: 8 (over y, core), gy: 32 (over z, x).
Axes of the slice: x: 4, y: 4, z: 8, core: 2. Of those that a mesh axis runs over, the one named last changes fastest.
Arguments:
- right_side: float32 [64, 256, 1024], P('gz', 'gy'), may hold values from -5 to 5
- coefficient: float32 [64, 256, 1024], P('gz', 'gy'), may hold values from 0.5 to 4
Outputs:
- correction: float32 [64, 256, 1024], P('gz', 'gy')
- residual: float32 [64, 256, 1024], P('gz', 'gy')
All inputs are finite; a program needn't handle non-finite values.
Results may differ from a plain program's by a relative error of at most 0.0003.
Values sent between devices are 32-bit elements; how exact they have to be, the bound alone decides.
A program may use at most 64 MiB of HBM per device.

v0:
```python
import jax
import jax.numpy as jnp
from jax import lax
from jax.sharding import PartitionSpec as P

LEVELS = 4


def extended(array, sides, width):
    for axis, dim in sides:
        size, length = (lax.axis_size(axis), array.shape[dim])
        up = [(i, (i + 1) % size) for i in range(size - 1)]
        down = [(j, i) for i, j in up]
        last = lax.slice_in_dim(array, length - width, length, axis=dim)
        initial = lax.slice_in_dim(array, 0, width, axis=dim)
        before = lax.ppermute(last, axis, up)
        after = lax.ppermute(initial, axis, down)
        array = jnp.concatenate([before, array, after], axis=dim)
    return array


def coarsen(field):
    total = field[0::2, 0::2, 0::2] + field[0::2, 0::2, 1::2]
    total = total + field[0::2, 1::2, 0::2] + field[0::2, 1::2, 1::2]
    total = total + field[1::2, 0::2, 0::2] + field[1::2, 0::2, 1::2]
    total = total + field[1::2, 1::2, 0::2] + field[1::2, 1::2, 1::2]
    return total * 0.125


def prolong(field):
    return jnp.repeat(jnp.repeat(jnp.repeat(field, 2, axis=0), 2, axis=1), 2, axis=2)


def face_terms(kpad):
    center = kpad[1:-1, 1:-1, 1:-1]
    z_minus = 0.5 * (center + kpad[:-2, 1:-1, 1:-1])
    z_plus = 0.5 * (center + kpad[2:, 1:-1, 1:-1])
    y_minus = 0.5 * (center + kpad[1:-1, :-2, 1:-1])
    y_plus = 0.5 * (center + kpad[1:-1, 2:, 1:-1])
    x_minus = 0.5 * (center + kpad[1:-1, 1:-1, :-2])
    x_plus = 0.5 * (center + kpad[1:-1, 1:-1, 2:])
    total = z_minus + z_plus + y_minus + y_plus + x_minus + x_plus
    return ((z_minus, z_plus, y_minus, y_plus, x_minus, x_plus), total)


def neighbour_sum(weights, upad):
    z_minus, z_plus, y_minus, y_plus, x_minus, x_plus = weights
    acc = z_minus * upad[:-2, 1:-1, 1:-1] + z_plus * upad[2:, 1:-1, 1:-1]
    acc = acc + y_minus * upad[1:-1, :-2, 1:-1] + y_plus * upad[1:-1, 2:, 1:-1]
    acc = acc + x_minus * upad[1:-1, 1:-1, :-2] + x_plus * upad[1:-1, 1:-1, 2:]
    return acc


def extend(field, layout):
    if layout == "column":
        wider = extended(field, (("gy", 1),), 1)
        wider = jnp.pad(wider, ((1, 1), (0, 0), (0, 0)))
    else:
        wider = extended(field, (("gz", 0), ("gy", 1)), 1)
    return jnp.pad(wider, ((0, 0), (0, 0), (1, 1)))


def region_masks(shape, z_start, y_start):
    zpos = lax.broadcasted_iota(jnp.int32, shape, 0) + z_start
    ypos = lax.broadcasted_iota(jnp.int32, shape, 1) + y_start
    xpos = lax.broadcasted_iota(jnp.int32, shape, 2)
    return (zpos + ypos + xpos + 4) % 2


def cycle(rhs, conduct, level, layout, z_start, y_start, z_total, y_total):
    scale = 4.0**level
    weights, total = face_terms(extend(conduct, layout))
    parity = region_masks(rhs.shape, z_start, y_start)
    first = parity == 0
    second = parity == 1

    def relax(field, colour):
        fresh = (scale * rhs + neighbour_sum(weights, extend(field, layout))) / total
        return jnp.where(colour, fresh, field)

    def smooth(field, sweeps):
        for sweep in range(sweeps):
            for colour in (first, second):
                field = relax(field, colour)
        return field

    def remainder(field):
        return rhs - (total * field - neighbour_sum(weights, extend(field, layout))) / scale

    field = jnp.zeros(rhs.shape, jnp.float32)
    if level == LEVELS - 1:
        return (smooth(field, 12), None)
    field = smooth(field, 2)
    rhs_next = coarsen(remainder(field))
    conduct_next = coarsen(conduct)
    joined = layout == "split" and level == 1
    if joined:
        local_depth = rhs_next.shape[0]
        rhs_next, conduct_next = (
            lax.all_gather(rhs_next, "gz", axis=0, tiled=True),
            lax.all_gather(conduct_next, "gz", axis=0, tiled=True),
        )
        error, unused = cycle(
            rhs_next, conduct_next, level + 1, "column", 0, y_start // 2, z_total // 2, y_total // 2
        )
        error = lax.dynamic_slice_in_dim(error, lax.axis_index("gz") * local_depth, local_depth, 0)
    else:
        error, unused = cycle(
            rhs_next,
            conduct_next,
            level + 1,
            layout,
            z_start // 2,
            y_start // 2,
            z_total // 2,
            y_total // 2,
        )
    field = field + prolong(error)
    field = smooth(field, 2)
    return (field, remainder(field))


def on_device(right_side, coefficient):
    depth, rows, width = right_side.shape
    z_start = lax.axis_index("gz") * depth
    y_start = lax.axis_index("gy") * rows
    z_total = depth * lax.axis_size("gz")
    y_total = rows * lax.axis_size("gy")
    correction, residual = cycle(
        right_side, coefficient, 0, "split", z_start, y_start, z_total, y_total
    )
    return (correction, residual)


def solution(mesh):
    placed = (P("gz", "gy", None), P("gz", "gy", None))
    return jax.shard_map(
        on_device,
        mesh=mesh,
        in_specs=placed,
        out_specs=(P("gz", "gy", None), P("gz", "gy", None)),
        check_vma=False,
    )
```

profile of v0, /device:TPU:103, one launch (start us, length us, event | category | flops | bytes accessed | tf_op | source)
XLA Modules:
  0.0 815.2 jit_solution(264475233416523704)
XLA Ops:
  17.4 6.1 collective-permute-start.4
  29.6 4.3 collective-permute-done.7
  36.3 5.8 collective-permute-start.8
  66.9 4.6 collective-permute-done.11
  72.5 3.8 collective-permute-start.12
  103.5 6.0 collective-permute-start.18
  113.4 6.7 collective-permute-start.28
  121.0 5.0 collective-permute-start.20
  137.6 5.5 collective-permute-done.23
  156.0 3.8 collective-permute-start.32
  163.7 6.7 collective-permute-start.62
  176.3 6.7 collective-permute-start.34
  185.0 5.8 collective-permute-done.35
  191.1 5.9 collective-permute-start.36
  198.9 13.0 %all_gather.7 = f32[16,2,256]{2,1,0:T(2,128)S(1)} all-gather(f32[2,2,256]{2,1,0:T(2,128)S(1)} %add_multiply_fusion.5), channel_id=1, replica_groups=mesh['gz'=8,'gy'=32] {'gz'}, dimensions={0}, use_global_device_ids=true | all-gather | bytes 36864 | tf_op jit(solution)/shard_map/all_gather | solution.py:101
  217.3 4.3 collective-permute-done.39
  234.5 5.2 collective-permute-start.42
  241.8 5.8 collective-permute-done.43
  247.9 5.4 collective-permute-start.44
  263.6 4.3 collective-permute-done.47
  272.2 13.0 %all_gather.6 = f32[16,2,256]{2,1,0:T(2,128)S(1)} all-gather(f32[2,2,256]{2,1,0:T(2,128)S(1)} %add_multiply_fusion.6), channel_id=1, replica_groups=mesh['gz'=8,'gy'=32] {'gz'}, dimensions={0}, use_global_device_ids=true | all-gather | bytes 36864 | tf_op jit(solution)/shard_map/all_gather | solution.py:100
  295.2 4.2 collective-permute-start.54
  301.4 6.7 collective-permute-start.60
  313.6 4.4 collective-permute-done.57
  323.5 4.6 collective-permute-done.59
  331.9 6.7 collective-permute-start.64
  341.3 6.9 collective-permute-start.66
  351.0 6.9 collective-permute-start.68
  360.7 6.9 collective-permute-start.70
  370.4 6.9 collective-permute-start.72
  380.1 6.9 collective-permute-start.74
  389.8 7.1 collective-permute-start.76
  399.6 6.9 collective-permute-start.78
  409.3 6.9 collective-permute-start.80
  419.0 6.9 collective-permute-start.82
  428.7 6.9 collective-permute-start.84
  438.3 6.9 collective-permute-start.86
  448.0 6.9 collective-permute-start.88
  457.7 6.9 collective-permute-start.90
  467.4 6.9 collective-permute-start.92
  477.1 6.9 collective-permute-start.94
  486.8 6.9 collective-permute-start.96
  496.5 6.9 collective-permute-start.98
  506.1 6.9 collective-permute-start.100
  515.8 6.9 collective-permute-start.102
  525.5 6.9 collective-permute-start.104
  535.2 6.9 collective-permute-start.106
  544.9 6.9 collective-permute-start.108
  552.9 6.9 collective-permute-start.110
  561.8 5.9 collective-permute-done.111
  573.1 4.4 collective-permute-done.113
  583.0 4.4 collective-permute-done.115
  592.9 4.3 collective-permute-done.117
  600.3 39.0 %collective-permute-start.118 = (f32[1,4,512]{2,1,0:T(4,128)S(1)}, f32[1,4,512]{2,1,0:T(4,128)S(1)}, u32[]{:S(2)}, u32[]{:S(2)}) collective-permute-start(f32[1,4,512]{2,1,0:T(4,128)S(1)} %get-tuple-element.111), channel_id=1, source_target_pairs={{0,32},{32,64},{64,96},{96,128},{128,160},{160,192},{192,224},{1,3... | collective-permute-start | bytes 24584 | tf_op jit(solution)/shard_map/ppermute | solution.py:16
  649.6 4.4 collective-permute-done.121
  667.7 4.4 collective-permute-done.125
  685.8 4.4 collective-permute-done.129
  704.0 4.4 collective-permute-done.133
  710.8 3.9 broadcast_in_dim.57
  731.2 4.7 collective-permute-done.137
  750.8 4.7 collective-permute-done.141
  770.1 4.7 collective-permute-done.145
  789.4 4.7 collective-permute-done.149
  808.7 4.7 collective-permute-done.153
  (499 shorter events, 394.3 us)
Async XLA Ops:
  0.7 22.9 %collective-permute-start.3 = (f32[1,8,1024]{2,1,0:T(8,128)S(1)}, f32[1,8,1024]{2,1,0:T(8,128)S(1)}, u32[]{:S(2)}, u32[]{:S(2)}) collective-permute-start(f32[1,8,1024]{2,1,0:T(8,128)S(1)} %broadcast.399), channel_id=1, source_target_pairs={{32,0},{64,32},{96,64},{128,96},{160,128},{192,160},{224,192},{33,... | collective-permute-start | bytes 98312 | tf_op jit(solution)/shard_map/ppermute | solution.py:17
  3.4 20.2 %collective-permute-start.1 = (f32[1,8,1024]{2,1,0:T(8,128)S(1)}, f32[1,8,1024]{2,1,0:T(8,128)S(1)}, u32[]{:S(2)}, u32[]{:S(2)}) collective-permute-start(f32[1,8,1024]{2,1,0:T(8,128)S(1)} %broadcast.399), channel_id=1, source_target_pairs={{0,32},{32,64},{64,96},{96,128},{128,160},{160,192},{192,224},{1,3... | collective-permute-start | bytes 98312 | tf_op jit(solution)/shard_map/ppermute | solution.py:16
  14.9 14.2 %collective-permute-start.6 = (f32[10,1,1024]{2,1,0:T(1,128)S(1)}, f32[10,1,1024]{2,1,0:T(1,128)S(1)}, u32[]{:S(2)}, u32[]{:S(2)}) collective-permute-start(f32[10,1,1024]{2,1,0:T(1,128)S(1)} %get-tuple-element.58), channel_id=1, source_target_pairs={{1,0},{2,1},{3,2},{4,3},{5,4},{6,5},{7,6},{8,7},{9,8},{10,9},{11,1... | collective-permute-start | bytes 122888 | tf_op jit(solution)/shard_map/ppermute | solution.py:17
  17.4 11.7 %collective-permute-start.4 = (f32[10,1,1024]{2,1,0:T(1,128)S(1)}, f32[10,1,1024]{2,1,0:T(1,128)S(1)}, u32[]{:S(2)}, u32[]{:S(2)}) collective-permute-start(f32[10,1,1024]{2,1,0:T(1,128)S(1)} %get-tuple-element.59), channel_id=1, source_target_pairs={{0,1},{1,2},{2,3},{3,4},{4,5},{5,6},{6,7},{7,8},{8,9},{9,10},{10,1... | collective-permute-start | bytes 122888 | tf_op jit(solution)/shard_map/ppermute | solution.py:16
  25.6 8.3 %collective-permute-start.7 = (f32[10,1,1024]{2,1,0:T(1,128)S(1)}, f32[10,1,1024]{2,1,0:T(1,128)S(1)}, u32[]{:S(2)}, u32[]{:S(2)}) collective-permute-start(f32[10,1,1024]{2,1,0:T(1,128)S(1)} %get-tuple-element.61), channel_id=1, source_target_pairs={{1,0},{2,1},{3,2},{4,3},{5,4},{6,5},{7,6},{8,7},{9,8},{10,9},{11,1... | collective-permute-start | bytes 122888 | tf_op jit(solution)/shard_map/ppermute | solution.py:17
  36.3 25.2 %collective-permute-start.8 = (f32[1,8,1024]{2,1,0:T(8,128)S(1)}, f32[1,8,1024]{2,1,0:T(8,128)S(1)}, u32[]{:S(2)}, u32[]{:S(2)}) collective-permute-start(f32[1,8,1024]{2,1,0:T(8,128)S(1)} %get-tuple-element.78), channel_id=1, source_target_pairs={{0,32},{32,64},{64,96},{96,128},{128,160},{160,192},{192,224},{1,3... | collective-permute-start | bytes 98312 | tf_op jit(solution)/shard_map/ppermute | solution.py:16
  42.1 19.4 %collective-permute-start.9 = (f32[1,8,1024]{2,1,0:T(8,128)S(1)}, f32[1,8,1024]{2,1,0:T(8,128)S(1)}, u32[]{:S(2)}, u32[]{:S(2)}) collective-permute-start(f32[1,8,1024]{2,1,0:T(8,128)S(1)} %get-tuple-element.79), channel_id=1, source_target_pairs={{32,0},{64,32},{96,64},{128,96},{160,128},{192,160},{224,192},{33,... | collective-permute-start | bytes 98312 | tf_op jit(solution)/shard_map/ppermute | solution.py:17
  44.0 52.1 %collective-permute-start.27 = (f32[1,4,512]{2,1,0:T(4,128)S(1)}, f32[1,4,512]{2,1,0:T(4,128)S(1)}, u32[]{:S(2)}, u32[]{:S(2)}) collective-permute-start(f32[1,4,512]{2,1,0:T(4,128)S(1)} %broadcast.402), channel_id=1, source_target_pairs={{32,0},{64,32},{96,64},{128,96},{160,128},{192,160},{224,192},{33,... | collective-permute-start | bytes 24584 | tf_op jit(solution)/shard_map/ppermute | solution.py:17
  46.0 52.1 %collective-permute-start.25 = (f32[1,4,512]{2,1,0:T(4,128)S(1)}, f32[1,4,512]{2,1,0:T(4,128)S(1)}, u32[]{:S(2)}, u32[]{:S(2)}) collective-permute-start(f32[1,4,512]{2,1,0:T(4,128)S(1)} %broadcast.402), channel_id=1, source_target_pairs={{0,32},{32,64},{64,96},{96,128},{128,160},{160,192},{192,224},{1,3... | collective-permute-start | bytes 24584 | tf_op jit(solution)/shard_map/ppermute | solution.py:16
  63.5 8.1 collective-permute-start.11
  78.2 31.2 %collective-permute-start.26 = (f32[1,4,512]{2,1,0:T(4,128)S(1)}, f32[1,4,512]{2,1,0:T(4,128)S(1)}, u32[]{:S(2)}, u32[]{:S(2)}) collective-permute-start(f32[1,4,512]{2,1,0:T(4,128)S(1)} %get-tuple-element.142), channel_id=1, source_target_pairs={{32,0},{64,32},{96,64},{128,96},{160,128},{192,160},{224,192},{33,... | collective-permute-start | bytes 24584 | tf_op jit(solution)/shard_map/ppermute | solution.py:17
  83.5 8.1 collective-permute-start.15
  86.9 24.5 %collective-permute-start.24 = (f32[1,4,512]{2,1,0:T(4,128)S(1)}, f32[1,4,512]{2,1,0:T(4,128)S(1)}, u32[]{:S(2)}, u32[]{:S(2)}) collective-permute-start(f32[1,4,512]{2,1,0:T(4,128)S(1)} %get-tuple-element.143), channel_id=1, source_target_pairs={{0,32},{32,64},{64,96},{96,128},{128,160},{160,192},{192,224},{1,3... | collective-permute-start | bytes 24584 | tf_op jit(solution)/shard_map/ppermute | solution.py:16
  92.5 8.2 %collective-permute-start.16 = (f32[1,8,1024]{2,1,0:T(8,128)S(1)}, f32[1,8,1024]{2,1,0:T(8,128)S(1)}, u32[]{:S(2)}, u32[]{:S(2)}) collective-permute-start(f32[1,8,1024]{2,1,0:T(8,128)S(1)} %get-tuple-element.74), channel_id=1, source_target_pairs={{0,32},{32,64},{64,96},{96,128},{128,160},{160,192},{192,224},{1,3... | collective-permute-start | bytes 98312 | tf_op jit(solution)/shard_map/ppermute | solution.py:16
  98.1 39.3 %collective-permute-start.29 = (f32[6,1,512]{2,1,0:T(1,128)S(1)}, f32[6,1,512]{2,1,0:T(1,128)S(1)}, u32[]{:S(2)}, u32[]{:S(2)}) collective-permute-start(f32[6,1,512]{2,1,0:T(1,128)S(1)} %get-tuple-element.103), channel_id=1, source_target_pairs={{0,1},{1,2},{2,3},{3,4},{4,5},{5,6},{6,7},{7,8},{8,9},{9,10},{10,1... | collective-permute-start | bytes 36872 | tf_op jit(solution)/shard_map/ppermute | solution.py:16
  100.8 36.7 %collective-permute-start.31 = (f32[6,1,512]{2,1,0:T(1,128)S(1)}, f32[6,1,512]{2,1,0:T(1,128)S(1)}, u32[]{:S(2)}, u32[]{:S(2)}) collective-permute-start(f32[6,1,512]{2,1,0:T(1,128)S(1)} %get-tuple-element.104), channel_id=1, source_target_pairs={{1,0},{2,1},{3,2},{4,3},{5,4},{6,5},{7,6},{8,7},{9,8},{10,9},{11,1... | collective-permute-start | bytes 36872 | tf_op jit(solution)/shard_map/ppermute | solution.py:17
  103.5 9.9 %collective-permute-start.18 = (f32[10,1,1024]{2,1,0:T(1,128)S(1)}, f32[10,1,1024]{2,1,0:T(1,128)S(1)}, u32[]{:S(2)}, u32[]{:S(2)}) collective-permute-start(f32[10,1,1024]{2,1,0:T(1,128)S(1)} %get-tuple-element.52), channel_id=1, source_target_pairs={{0,1},{1,2},{2,3},{3,4},{4,5},{5,6},{6,7},{7,8},{8,9},{9,10},{10,1... | collective-permute-start | bytes 122888 | tf_op jit(solution)/shard_map/ppermute | solution.py:16
  109.5 10.6 %collective-permute-start.19 = (f32[10,1,1024]{2,1,0:T(1,128)S(1)}, f32[10,1,1024]{2,1,0:T(1,128)S(1)}, u32[]{:S(2)}, u32[]{:S(2)}) collective-permute-start(f32[10,1,1024]{2,1,0:T(1,128)S(1)} %get-tuple-element.53), channel_id=1, source_target_pairs={{1,0},{2,1},{3,2},{4,3},{5,4},{6,5},{7,6},{8,7},{9,8},{10,9},{11,1... | collective-permute-start | bytes 122888 | tf_op jit(solution)/shard_map/ppermute | solution.py:17
  111.4 14.6 %collective-permute-start.30 = (f32[6,1,512]{2,1,0:T(1,128)S(1)}, f32[6,1,512]{2,1,0:T(1,128)S(1)}, u32[]{:S(2)}, u32[]{:S(2)}) collective-permute-start(f32[6,1,512]{2,1,0:T(1,128)S(1)} %get-tuple-element.101), channel_id=1, source_target_pairs={{1,0},{2,1},{3,2},{4,3},{5,4},{6,5},{7,6},{8,7},{9,8},{10,9},{11,1... | collective-permute-start | bytes 36872 | tf_op jit(solution)/shard_map/ppermute | solution.py:17
  113.4 14.6 %collective-permute-start.28 = (f32[6,1,512]{2,1,0:T(1,128)S(1)}, f32[6,1,512]{2,1,0:T(1,128)S(1)}, u32[]{:S(2)}, u32[]{:S(2)}) collective-permute-start(f32[6,1,512]{2,1,0:T(1,128)S(1)} %get-tuple-element.102), channel_id=1, source_target_pairs={{0,1},{1,2},{2,3},{3,4},{4,5},{5,6},{6,7},{7,8},{8,9},{9,10},{10,1... | collective-permute-start | bytes 36872 | tf_op jit(solution)/shard_map/ppermute | solution.py:16
  135.0 8.1 collective-permute-start.23
  156.0 20.2 %collective-permute-start.32 = (f32[1,4,512]{2,1,0:T(4,128)S(1)}, f32[1,4,512]{2,1,0:T(4,128)S(1)}, u32[]{:S(2)}, u32[]{:S(2)}) collective-permute-start(f32[1,4,512]{2,1,0:T(4,128)S(1)} %get-tuple-element.140), channel_id=1, source_target_pairs={{0,32},{32,64},{64,96},{96,128},{128,160},{160,192},{192,224},{1,3... | collective-permute-start | bytes 24584 | tf_op jit(solution)/shard_map/ppermute | solution.py:16
  159.8 16.5 %collective-permute-start.33 = (f32[1,4,512]{2,1,0:T(4,128)S(1)}, f32[1,4,512]{2,1,0:T(4,128)S(1)}, u32[]{:S(2)}, u32[]{:S(2)}) collective-permute-start(f32[1,4,512]{2,1,0:T(4,128)S(1)} %get-tuple-element.141), channel_id=1, source_target_pairs={{32,0},{64,32},{96,64},{128,96},{160,128},{192,160},{224,192},{33,... | collective-permute-start | bytes 24584 | tf_op jit(solution)/shard_map/ppermute | solution.py:17
  161.7 148.5 %collective-permute-start.63 = (f32[8,1,128]{2,0,1:T(8,128)S(1)}, f32[8,1,128]{2,0,1:T(8,128)S(1)}, u32[]{:S(2)}, u32[]{:S(2)}) collective-permute-start(f32[8,1,128]{2,0,1:T(8,128)S(1)} %broadcast_in_dim.46), channel_id=1, source_target_pairs={{1,0},{2,1},{3,2},{4,3},{5,4},{6,5},{7,6},{8,7},{9,8},{10,9},{11,1... | collective-permute-start | bytes 12296 | tf_op jit(solution)/shard_map/ppermute | solution.py:17
  163.7 149.9 %collective-permute-start.62 = (f32[8,1,128]{2,0,1:T(8,128)S(1)}, f32[8,1,128]{2,0,1:T(8,128)S(1)}, u32[]{:S(2)}, u32[]{:S(2)}) collective-permute-start(f32[8,1,128]{2,0,1:T(8,128)S(1)} %broadcast_in_dim.46), channel_id=1, source_target_pairs={{0,1},{1,2},{2,3},{3,4},{4,5},{5,6},{6,7},{7,8},{8,9},{9,10},{10,1... | collective-permute-start | bytes 12296 | tf_op jit(solution)/shard_map/ppermute | solution.py:16
  170.4 89.8 %collective-permute-start.51 = (f32[16,1,256]{2,0,1:T(8,128)S(1)}, f32[16,1,256]{2,0,1:T(8,128)S(1)}, u32[]{:S(2)}, u32[]{:S(2)}) collective-permute-start(f32[16,1,256]{2,0,1:T(8,128)S(1)} %broadcast.408), channel_id=1, source_target_pairs={{1,0},{2,1},{3,2},{4,3},{5,4},{6,5},{7,6},{8,7},{9,8},{10,9},{11,1... | collective-permute-start | bytes 49160 | tf_op jit(solution)/shard_map/ppermute | solution.py:17
  176.3 8.6 %collective-permute-start.34 = (f32[6,1,512]{2,1,0:T(1,128)S(1)}, f32[6,1,512]{2,1,0:T(1,128)S(1)}, u32[]{:S(2)}, u32[]{:S(2)}) collective-permute-start(f32[6,1,512]{2,1,0:T(1,128)S(1)} %get-tuple-element.99), channel_id=1, source_target_pairs={{0,1},{1,2},{2,3},{3,4},{4,5},{5,6},{6,7},{7,8},{8,9},{9,10},{10,1... | collective-permute-start | bytes 36872 | tf_op jit(solution)/shard_map/ppermute | solution.py:16
  191.1 20.8 %collective-permute-start.36 = (f32[1,4,512]{2,1,0:T(4,128)S(1)}, f32[1,4,512]{2,1,0:T(4,128)S(1)}, u32[]{:S(2)}, u32[]{:S(2)}) collective-permute-start(f32[1,4,512]{2,1,0:T(4,128)S(1)} %get-tuple-element.138), channel_id=1, source_target_pairs={{0,32},{32,64},{64,96},{96,128},{128,160},{160,192},{192,224},{1,3... | collective-permute-start | bytes 24584 | tf_op jit(solution)/shard_map/ppermute | solution.py:16
  197.0 14.9 %collective-permute-start.37 = (f32[1,4,512]{2,1,0:T(4,128)S(1)}, f32[1,4,512]{2,1,0:T(4,128)S(1)}, u32[]{:S(2)}, u32[]{:S(2)}) collective-permute-start(f32[1,4,512]{2,1,0:T(4,128)S(1)} %get-tuple-element.139), channel_id=1, source_target_pairs={{32,0},{64,32},{96,64},{128,96},{160,128},{192,160},{224,192},{33,... | collective-permute-start | bytes 24584 | tf_op jit(solution)/shard_map/ppermute | solution.py:17
  231.1 8.7 %collective-permute-start.49 = (f32[16,1,256]{2,0,1:T(8,128)S(1)}, f32[16,1,256]{2,0,1:T(8,128)S(1)}, u32[]{:S(2)}, u32[]{:S(2)}) collective-permute-start(f32[16,1,256]{2,0,1:T(8,128)S(1)} %get-tuple-element.135), channel_id=1, source_target_pairs={{1,0},{2,1},{3,2},{4,3},{5,4},{6,5},{7,6},{8,7},{9,8},{10,9},{11,1... | collective-permute-start | bytes 49160 | tf_op jit(solution)/shard_map/ppermute | solution.py:17
  255.3 8.3 %collective-permute-start.50 = (f32[16,1,256]{2,0,1:T(8,128)S(1)}, f32[16,1,256]{2,0,1:T(8,128)S(1)}, u32[]{:S(2)}, u32[]{:S(2)}) collective-permute-start(f32[16,1,256]{2,0,1:T(8,128)S(1)} %broadcast.408), channel_id=1, source_target_pairs={{0,1},{1,2},{2,3},{3,4},{4,5},{5,6},{6,7},{7,8},{8,9},{9,10},{10,1... | collective-permute-start | bytes 49160 | tf_op jit(solution)/shard_map/ppermute | solution.py:16
  290.7 32.8 %collective-permute-start.61 = (f32[8,1,128]{2,0,1:T(8,128)S(1)}, f32[8,1,128]{2,0,1:T(8,128)S(1)}, u32[]{:S(2)}, u32[]{:S(2)}) collective-permute-start(f32[8,1,128]{2,0,1:T(8,128)S(1)} %add_multiply_fusion.3), channel_id=1, source_target_pairs={{1,0},{2,1},{3,2},{4,3},{5,4},{6,5},{7,6},{8,7},{9,8},{10,9},{11,1... | collective-permute-start | bytes 12296 | tf_op jit(solution)/shard_map/ppermute | solution.py:17
  299.5 8.6 %collective-permute-start.55 = (f32[16,1,256]{2,0,1:T(8,128)S(1)}, f32[16,1,256]{2,0,1:T(8,128)S(1)}, u32[]{:S(2)}, u32[]{:S(2)}) collective-permute-start(f32[16,1,256]{2,0,1:T(8,128)S(1)} %get-tuple-element.129), channel_id=1, source_target_pairs={{1,0},{2,1},{3,2},{4,3},{5,4},{6,5},{7,6},{8,7},{9,8},{10,9},{11,1... | collective-permute-start | bytes 49160 | tf_op jit(solution)/shard_map/ppermute | solution.py:17
  301.4 22.0 %collective-permute-start.60 = (f32[8,1,128]{2,0,1:T(8,128)S(1)}, f32[8,1,128]{2,0,1:T(8,128)S(1)}, u32[]{:S(2)}, u32[]{:S(2)}) collective-permute-start(f32[8,1,128]{2,0,1:T(8,128)S(1)} %add_multiply_fusion.3), channel_id=1, source_target_pairs={{0,1},{1,2},{2,3},{3,4},{4,5},{5,6},{6,7},{7,8},{8,9},{9,10},{10,1... | collective-permute-start | bytes 12296 | tf_op jit(solution)/shard_map/ppermute | solution.py:16
  330.0 8.6 %collective-permute-start.65 = (f32[8,1,128]{2,0,1:T(8,128)S(1)}, f32[8,1,128]{2,0,1:T(8,128)S(1)}, u32[]{:S(2)}, u32[]{:S(2)}) collective-permute-start(f32[8,1,128]{2,0,1:T(8,128)S(1)} %get-tuple-element.21), channel_id=1, source_target_pairs={{1,0},{2,1},{3,2},{4,3},{5,4},{6,5},{7,6},{8,7},{9,8},{10,9},{11,1... | collective-permute-start | bytes 12296 | tf_op jit(solution)/shard_map/ppermute | solution.py:17
  339.4 8.9 %collective-permute-start.67 = (f32[8,1,128]{2,0,1:T(8,128)S(1)}, f32[8,1,128]{2,0,1:T(8,128)S(1)}, u32[]{:S(2)}, u32[]{:S(2)}) collective-permute-start(f32[8,1,128]{2,0,1:T(8,128)S(1)} %fusion.383), channel_id=1, source_target_pairs={{1,0},{2,1},{3,2},{4,3},{5,4},{6,5},{7,6},{8,7},{9,8},{10,9},{11,1... | collective-permute-start | bytes 12296 | tf_op jit(solution)/shard_map/ppermute | solution.py:17
  349.1 8.9 %collective-permute-start.69 = (f32[8,1,128]{2,0,1:T(8,128)S(1)}, f32[8,1,128]{2,0,1:T(8,128)S(1)}, u32[]{:S(2)}, u32[]{:S(2)}) collective-permute-start(f32[8,1,128]{2,0,1:T(8,128)S(1)} %fusion.390), channel_id=1, source_target_pairs={{1,0},{2,1},{3,2},{4,3},{5,4},{6,5},{7,6},{8,7},{9,8},{10,9},{11,1... | collective-permute-start | bytes 12296 | tf_op jit(solution)/shard_map/ppermute | solution.py:17
  358.8 8.9 %collective-permute-start.71 = (f32[8,1,128]{2,0,1:T(8,128)S(1)}, f32[8,1,128]{2,0,1:T(8,128)S(1)}, u32[]{:S(2)}, u32[]{:S(2)}) collective-permute-start(f32[8,1,128]{2,0,1:T(8,128)S(1)} %fusion.397), channel_id=1, source_target_pairs={{1,0},{2,1},{3,2},{4,3},{5,4},{6,5},{7,6},{8,7},{9,8},{10,9},{11,1... | collective-permute-start | bytes 12296 | tf_op jit(solution)/shard_map/ppermute | solution.py:17
  368.5 8.9 %collective-permute-start.73 = (f32[8,1,128]{2,0,1:T(8,128)S(1)}, f32[8,1,128]{2,0,1:T(8,128)S(1)}, u32[]{:S(2)}, u32[]{:S(2)}) collective-permute-start(f32[8,1,128]{2,0,1:T(8,128)S(1)} %fusion.404), channel_id=1, source_target_pairs={{1,0},{2,1},{3,2},{4,3},{5,4},{6,5},{7,6},{8,7},{9,8},{10,9},{11,1... | collective-permute-start | bytes 12296 | tf_op jit(solution)/shard_map/ppermute | solution.py:17
  378.2 8.9 %collective-permute-start.75 = (f32[8,1,128]{2,0,1:T(8,128)S(1)}, f32[8,1,128]{2,0,1:T(8,128)S(1)}, u32[]{:S(2)}, u32[]{:S(2)}) collective-permute-start(f32[8,1,128]{2,0,1:T(8,128)S(1)} %fusion.411), channel_id=1, source_target_pairs={{1,0},{2,1},{3,2},{4,3},{5,4},{6,5},{7,6},{8,7},{9,8},{10,9},{11,1... | collective-permute-start | bytes 12296 | tf_op jit(solution)/shard_map/ppermute | solution.py:17
  387.9 9.0 %collective-permute-start.77 = (f32[8,1,128]{2,0,1:T(8,128)S(1)}, f32[8,1,128]{2,0,1:T(8,128)S(1)}, u32[]{:S(2)}, u32[]{:S(2)}) collective-permute-start(f32[8,1,128]{2,0,1:T(8,128)S(1)} %fusion.418), channel_id=1, source_target_pairs={{1,0},{2,1},{3,2},{4,3},{5,4},{6,5},{7,6},{8,7},{9,8},{10,9},{11,1... | collective-permute-start | bytes 12296 | tf_op jit(solution)/shard_map/ppermute | solution.py:17
  397.7 8.9 %collective-permute-start.79 = (f32[8,1,128]{2,0,1:T(8,128)S(1)}, f32[8,1,128]{2,0,1:T(8,128)S(1)}, u32[]{:S(2)}, u32[]{:S(2)}) collective-permute-start(f32[8,1,128]{2,0,1:T(8,128)S(1)} %fusion.425), channel_id=1, source_target_pairs={{1,0},{2,1},{3,2},{4,3},{5,4},{6,5},{7,6},{8,7},{9,8},{10,9},{11,1... | collective-permute-start | bytes 12296 | tf_op jit(solution)/shard_map/ppermute | solution.py:17
  407.4 8.9 %collective-permute-start.81 = (f32[8,1,128]{2,0,1:T(8,128)S(1)}, f32[8,1,128]{2,0,1:T(8,128)S(1)}, u32[]{:S(2)}, u32[]{:S(2)}) collective-permute-start(f32[8,1,128]{2,0,1:T(8,128)S(1)} %fusion.432), channel_id=1, source_target_pairs={{1,0},{2,1},{3,2},{4,3},{5,4},{6,5},{7,6},{8,7},{9,8},{10,9},{11,1... | collective-permute-start | bytes 12296 | tf_op jit(solution)/shard_map/ppermute | solution.py:17
  417.0 8.9 %collective-permute-start.83 = (f32[8,1,128]{2,0,1:T(8,128)S(1)}, f32[8,1,128]{2,0,1:T(8,128)S(1)}, u32[]{:S(2)}, u32[]{:S(2)}) collective-permute-start(f32[8,1,128]{2,0,1:T(8,128)S(1)} %fusion.439), channel_id=1, source_target_pairs={{1,0},{2,1},{3,2},{4,3},{5,4},{6,5},{7,6},{8,7},{9,8},{10,9},{11,1... | collective-permute-start | bytes 12296 | tf_op jit(solution)/shard_map/ppermute | solution.py:17
  426.7 8.9 %collective-permute-start.85 = (f32[8,1,128]{2,0,1:T(8,128)S(1)}, f32[8,1,128]{2,0,1:T(8,128)S(1)}, u32[]{:S(2)}, u32[]{:S(2)}) collective-permute-start(f32[8,1,128]{2,0,1:T(8,128)S(1)} %fusion.446), channel_id=1, source_target_pairs={{1,0},{2,1},{3,2},{4,3},{5,4},{6,5},{7,6},{8,7},{9,8},{10,9},{11,1... | collective-permute-start | bytes 12296 | tf_op jit(solution)/shard_map/ppermute | solution.py:17
  436.4 8.9 %collective-permute-start.87 = (f32[8,1,128]{2,0,1:T(8,128)S(1)}, f32[8,1,128]{2,0,1:T(8,128)S(1)}, u32[]{:S(2)}, u32[]{:S(2)}) collective-permute-start(f32[8,1,128]{2,0,1:T(8,128)S(1)} %fusion.453), channel_id=1, source_target_pairs={{1,0},{2,1},{3,2},{4,3},{5,4},{6,5},{7,6},{8,7},{9,8},{10,9},{11,1... | collective-permute-start | bytes 12296 | tf_op jit(solution)/shard_map/ppermute | solution.py:17
  446.1 8.9 %collective-permute-start.89 = (f32[8,1,128]{2,0,1:T(8,128)S(1)}, f32[8,1,128]{2,0,1:T(8,128)S(1)}, u32[]{:S(2)}, u32[]{:S(2)}) collective-permute-start(f32[8,1,128]{2,0,1:T(8,128)S(1)} %fusion.460), channel_id=1, source_target_pairs={{1,0},{2,1},{3,2},{4,3},{5,4},{6,5},{7,6},{8,7},{9,8},{10,9},{11,1... | collective-permute-start | bytes 12296 | tf_op jit(solution)/shard_map/ppermute | solution.py:17
  455.8 8.9 %collective-permute-start.91 = (f32[8,1,128]{2,0,1:T(8,128)S(1)}, f32[8,1,128]{2,0,1:T(8,128)S(1)}, u32[]{:S(2)}, u32[]{:S(2)}) collective-permute-start(f32[8,1,128]{2,0,1:T(8,128)S(1)} %fusion.467), channel_id=1, source_target_pairs={{1,0},{2,1},{3,2},{4,3},{5,4},{6,5},{7,6},{8,7},{9,8},{10,9},{11,1... | collective-permute-start | bytes 12296 | tf_op jit(solution)/shard_map/ppermute | solution.py:17
  465.5 8.9 %collective-permute-start.93 = (f32[8,1,128]{2,0,1:T(8,128)S(1)}, f32[8,1,128]{2,0,1:T(8,128)S(1)}, u32[]{:S(2)}, u32[]{:S(2)}) collective-permute-start(f32[8,1,128]{2,0,1:T(8,128)S(1)} %fusion.474), channel_id=1, source_target_pairs={{1,0},{2,1},{3,2},{4,3},{5,4},{6,5},{7,6},{8,7},{9,8},{10,9},{11,1... | collective-permute-start | bytes 12296 | tf_op jit(solution)/shard_map/ppermute | solution.py:17
  475.2 8.9 %collective-permute-start.95 = (f32[8,1,128]{2,0,1:T(8,128)S(1)}, f32[8,1,128]{2,0,1:T(8,128)S(1)}, u32[]{:S(2)}, u32[]{:S(2)}) collective-permute-start(f32[8,1,128]{2,0,1:T(8,128)S(1)} %fusion.481), channel_id=1, source_target_pairs={{1,0},{2,1},{3,2},{4,3},{5,4},{6,5},{7,6},{8,7},{9,8},{10,9},{11,1... | collective-permute-start | bytes 12296 | tf_op jit(solution)/shard_map/ppermute | solution.py:17
  484.9 8.9 %collective-permute-start.97 = (f32[8,1,128]{2,0,1:T(8,128)S(1)}, f32[8,1,128]{2,0,1:T(8,128)S(1)}, u32[]{:S(2)}, u32[]{:S(2)}) collective-permute-start(f32[8,1,128]{2,0,1:T(8,128)S(1)} %fusion.488), channel_id=1, source_target_pairs={{1,0},{2,1},{3,2},{4,3},{5,4},{6,5},{7,6},{8,7},{9,8},{10,9},{11,1... | collective-permute-start | bytes 12296 | tf_op jit(solution)/shard_map/ppermute | solution.py:17
  494.5 8.9 %collective-permute-start.99 = (f32[8,1,128]{2,0,1:T(8,128)S(1)}, f32[8,1,128]{2,0,1:T(8,128)S(1)}, u32[]{:S(2)}, u32[]{:S(2)}) collective-permute-start(f32[8,1,128]{2,0,1:T(8,128)S(1)} %fusion.495), channel_id=1, source_target_pairs={{1,0},{2,1},{3,2},{4,3},{5,4},{6,5},{7,6},{8,7},{9,8},{10,9},{11,1... | collective-permute-start | bytes 12296 | tf_op jit(solution)/shard_map/ppermute | solution.py:17
  504.2 8.9 %collective-permute-start.101 = (f32[8,1,128]{2,0,1:T(8,128)S(1)}, f32[8,1,128]{2,0,1:T(8,128)S(1)}, u32[]{:S(2)}, u32[]{:S(2)}) collective-permute-start(f32[8,1,128]{2,0,1:T(8,128)S(1)} %fusion.502), channel_id=1, source_target_pairs={{1,0},{2,1},{3,2},{4,3},{5,4},{6,5},{7,6},{8,7},{9,8},{10,9},{11,1... | collective-permute-start | bytes 12296 | tf_op jit(solution)/shard_map/ppermute | solution.py:17
  513.9 8.9 %collective-permute-start.103 = (f32[8,1,128]{2,0,1:T(8,128)S(1)}, f32[8,1,128]{2,0,1:T(8,128)S(1)}, u32[]{:S(2)}, u32[]{:S(2)}) collective-permute-start(f32[8,1,128]{2,0,1:T(8,128)S(1)} %fusion.509), channel_id=1, source_target_pairs={{1,0},{2,1},{3,2},{4,3},{5,4},{6,5},{7,6},{8,7},{9,8},{10,9},{11,1... | collective-permute-start | bytes 12296 | tf_op jit(solution)/shard_map/ppermute | solution.py:17
  523.6 8.9 %collective-permute-start.105 = (f32[8,1,128]{2,0,1:T(8,128)S(1)}, f32[8,1,128]{2,0,1:T(8,128)S(1)}, u32[]{:S(2)}, u32[]{:S(2)}) collective-permute-start(f32[8,1,128]{2,0,1:T(8,128)S(1)} %fusion.516), channel_id=1, source_target_pairs={{1,0},{2,1},{3,2},{4,3},{5,4},{6,5},{7,6},{8,7},{9,8},{10,9},{11,1... | collective-permute-start | bytes 12296 | tf_op jit(solution)/shard_map/ppermute | solution.py:17
  533.3 8.9 %collective-permute-start.107 = (f32[8,1,128]{2,0,1:T(8,128)S(1)}, f32[8,1,128]{2,0,1:T(8,128)S(1)}, u32[]{:S(2)}, u32[]{:S(2)}) collective-permute-start(f32[8,1,128]{2,0,1:T(8,128)S(1)} %fusion.523), channel_id=1, source_target_pairs={{1,0},{2,1},{3,2},{4,3},{5,4},{6,5},{7,6},{8,7},{9,8},{10,9},{11,1... | collective-permute-start | bytes 12296 | tf_op jit(solution)/shard_map/ppermute | solution.py:17
  543.0 8.9 %collective-permute-start.109 = (f32[8,1,128]{2,0,1:T(8,128)S(1)}, f32[8,1,128]{2,0,1:T(8,128)S(1)}, u32[]{:S(2)}, u32[]{:S(2)}) collective-permute-start(f32[8,1,128]{2,0,1:T(8,128)S(1)} %fusion.530), channel_id=1, source_target_pairs={{1,0},{2,1},{3,2},{4,3},{5,4},{6,5},{7,6},{8,7},{9,8},{10,9},{11,1... | collective-permute-start | bytes 12296 | tf_op jit(solution)/shard_map/ppermute | solution.py:17
  552.9 8.9 %collective-permute-start.110 = (f32[16,1,256]{2,0,1:T(8,128)S(1)}, f32[16,1,256]{2,0,1:T(8,128)S(1)}, u32[]{:S(2)}, u32[]{:S(2)}) collective-permute-start(f32[16,1,256]{2,0,1:T(8,128)S(1)} %get-tuple-element.122), channel_id=1, source_target_pairs={{0,1},{1,2},{2,3},{3,4},{4,5},{5,6},{6,7},{7,8},{8,9},{9,10},{10,1... | collective-permute-start | bytes 49160 | tf_op jit(solution)/shard_map/ppermute | solution.py:16
  600.3 41.0 %collective-permute-start.118 = (f32[1,4,512]{2,1,0:T(4,128)S(1)}, f32[1,4,512]{2,1,0:T(4,128)S(1)}, u32[]{:S(2)}, u32[]{:S(2)}) collective-permute-start(f32[1,4,512]{2,1,0:T(4,128)S(1)} %get-tuple-element.111), channel_id=1, source_target_pairs={{0,32},{32,64},{64,96},{96,128},{128,160},{160,192},{192,224},{1,3... | collective-permute-start | bytes 24584 | tf_op jit(solution)/shard_map/ppermute | solution.py:16
  727.9 8.1 collective-permute-start.137
  747.4 8.1 collective-permute-start.141
  766.7 8.1 collective-permute-start.145
  786.0 8.1 collective-permute-start.149
  805.4 8.1 collective-permute-start.153
  (93 other events, 698.8 us)
where the time goes:
time: 827 us; the launch traced here: 815 us
  starting transfers between devices  558 us (67%)
  waiting for transfers between devices  160 us (19%)
  local copies, waits for them, and re-layouts  48.6 us (6%)
  blocking collectives  26 us (3%)
  other arithmetic  19 us (2%)
    ppermute x77, starting transfers between devices, extended(): before = lax.ppermute(last, axis, up)  377 us
    ppermute x77, starting transfers between devices, extended(): after = lax.ppermute(initial, axis, down)  180 us
    ppermute x77, waiting for transfers between devices, extended(): after = lax.ppermute(initial, axis, down)  142 us
    ppermute x77, waiting for transfers between devices, extended(): before = lax.ppermute(last, axis, up)  17.7 us
  transfers between devices with their start and end apart: 154, of which 60 were waited for; matrix products, arithmetic and copies ran while one was open for 4% of the time, Pallas kernels for 0%

commit v1 on v0

v1 whole, which is shorter than its diff:
```python
import jax
import jax.numpy as jnp
from jax import lax
from jax.experimental import pallas as pl
from jax.experimental.pallas import tpu as pltpu
from jax.sharding import PartitionSpec as P

MESH = pl.DeviceIdType.MESH
F32 = jnp.float32
T8 = (8, 128)

BUFFERS = dict(
    stage_f=(8, 8), stage_k=(8, 8),
    k0=(2, 10, 20), f0=(2, 8, 16), w0=(2, 6, 8, 16), d0=(2, 8, 16), g0=(2, 8, 16), r0=(10, 20), b0=(10, 20), p0=(10, 20),
    s0=(4, 8),
    c1k=(10, 20), c1f=(10, 20), k1=(2, 10, 20), w1=(2, 6, 8, 16), d1=(2, 8, 16), g1=(2, 8, 16), r1=(10, 20), b1=(10, 20), p1=(10, 20),
    s1=(2, 4),
    m2k=(9, 8), m2f=(9, 8), k2=(2, 20, 2), w2=(2, 6, 18, 2), d2=(2, 18, 2), g2=(2, 18, 2), r2=(20, 2), b2=(20, 2), p2=(20, 2),
    e2v=(10, 2, 2, 3), e2x=(10, 10),
    m3k=(32,), m3f=(32,), k3=(2, 18), w3=(2, 6, 16), d3=(2, 16), g3=(2, 16), r3=(18,), b3=(18,), e3=(40,),
)
ZEROED = ("k0", "f0", "r0", "b0", "p0", "c1k", "c1f", "r1", "b1", "p1", "k2", "r2", "b2", "p2", "e2v", "k3", "r3", "b3", "e3")
GROUPS = ("h0", "k1", "k2", "f1", "f1x", "u0", "u1", "k3", "f2", "f2x", "u2", "f3")


def iota(dim):
    return lax.broadcasted_iota(jnp.int32, T8, dim)


def nearest(d, n, size):
    if d == 0:
        return 0, 0, size
    if d > 0:
        return size - n, -d * size + size - n, n
    return 0, -d * size, n


def loop(first, end, body):
    def shifted(i, c):
        body(i - 8, c)
        return c

    lax.fori_loop(first + 8, end + 8, shifted, 0)


def kernel(nz, ny, f_in, k_in, u_out, r_out, *scratch):
    B = dict(zip(BUFFERS, scratch))
    in_sem, send_sem, recv_sem = scratch[len(BUFFERS):]
    gz, gy = lax.axis_index("gz"), lax.axis_index("gy")
    lane, sub = iota(1), iota(0)
    sent = dict.fromkeys(GROUPS, 0)

    def device(dz, dy):
        return (lax.rem(gz + (dz + nz) % nz, nz), lax.rem(gy + (dy + ny) % ny, ny))

    def pieces(hbm, ref, sem, out):
        copies = []
        for t in range(8):
            here, there = hbm.at[:, :, pl.ds(t * 128, 128)], ref.at[:, t]
            copies.append(pltpu.make_async_copy(there, here, sem) if out else pltpu.make_async_copy(here, there, sem))
        return copies

    def wait_bytes(sem, n):
        view = B["w0"].reshape(1536, 8, 128).at[pl.ds(0, n)]
        pltpu.make_async_copy(view, view, sem).wait()

    for c in pieces(k_in, B["stage_k"], in_sem.at[0], False) + pieces(f_in, B["stage_f"], in_sem.at[1], False):
        c.start()

    for name in ZEROED:
        shape = BUFFERS[name]
        ref = B[name]
        if len(shape) == 3 and shape[0] == 2:
            for i in range(2):
                def clear2(j, c, ref=ref, i=i, shape=shape):
                    ref[i, j] = jnp.zeros(shape[2:] + T8, F32)
                    return c
                lax.fori_loop(0, shape[1], clear2, 0)
        else:
            def clear(j, c, ref=ref, shape=shape):
                if shape[-1] == 3:
                    ref[j] = jnp.zeros((2, 2, 24, 128), F32)
                else:
                    ref[j] = jnp.zeros(shape[1:] + T8, F32)
                return c
            lax.fori_loop(0, shape[0], clear, 0)

    ring = [(a, b) for a in (-1, 0, 1) for b in (-1, 0, 1) if (a, b) != (0, 0)]
    far = [(2, 0), (-2, 0), (0, 2), (0, -2)]
    knights = [(a, b) for a in (-2, -1, 1, 2) for b in (-2, -1, 1, 2) if abs(a) != abs(b)]
    patch = [(a, b) for b in range(-4, 5) for a in range(nz) if (a, b) != (0, 0)]
    line = [b for b in range(1, ny)]
    everyone = patch + [(0, b) for b in line if 4 < b < ny - 4]
    barrier = pltpu.get_barrier_semaphore()
    for dz, dy in everyone:
        pl.semaphore_signal(barrier, inc=1, device_id=device(dz, dy), device_id_type=MESH)

    def put(group, src, dst, n, dz, dy):
        i = GROUPS.index(group)
        sent[group] += n
        pltpu.make_async_remote_copy(
            src_ref=src, dst_ref=dst, send_sem=send_sem.at[i], recv_sem=recv_sem.at[i],
            device_id=device(dz, dy), device_id_type=MESH,
        ).start()

    def received(group):
        wait_bytes(recv_sem.at[GROUPS.index(group)], sent[group])

    def finished(group):
        wait_bytes(send_sem.at[GROUPS.index(group)], sent[group])

    def packed(stage, dst, oq, oy):
        rows = B[stage].reshape(512, 128)
        target = B[dst]

        def body(y, c):
            even = (lane + y) & 1 == 0
            for q in range(4):
                lo = rows[pl.ds(2 * q * 64 + y, 8, stride=8), :]
                hi = rows[pl.ds((2 * q + 1) * 64 + y, 8, stride=8), :]
                target[0, q + oq, y + oy] = jnp.where(even, lo, hi)
                target[1, q + oq, y + oy] = jnp.where(even, hi, lo)
            return c

        lax.fori_loop(0, 8, body, 0)

    wait_bytes(in_sem.at[0], 64)
    packed("stage_k", "k0", 3, 6)
    wait_bytes(in_sem.at[1], 64)
    packed("stage_f", "f0", 2, 4)
    pl.semaphore_wait(barrier, len(everyone))

    def put0(group, name, oq, oy, colours, dz, dy, nq, nyy, skip_q=0):
        sq, tq, lq = nearest(dz, nq, 4)
        sy, ty, ly = nearest(dy, nyy, 8)
        if skip_q:
            lq = nq - skip_q
            if dz < 0:
                sq, tq = sq + skip_q, tq + skip_q
        ref = B[name]
        src, dst = (
            (pl.ds(sq + oq, lq), pl.ds(sy + oy, ly)),
            (pl.ds(tq + oq, lq), pl.ds(ty + oy, ly)),
        )
        if colours:
            put(group, ref.at[(slice(None),) + src], ref.at[(slice(None),) + dst], 2 * lq * ly, dz, dy)
        else:
            put(group, ref.at[src], ref.at[dst], lq * ly, dz, dy)

    def halo0(group, name, oq, oy, colours, depth):
        for dz, dy in ((0, 1), (0, -1), (1, 0), (-1, 0)):
            put0(group, name, oq, oy, colours, dz, dy, (depth + 1) // 2, depth)
        for dz, dy in ((1, 1), (1, -1), (-1, 1), (-1, -1)):
            put0(group, name, oq, oy, colours, dz, dy, 1, depth - 1)
            put0(group, name, oq, oy, colours, dz, dy, 2, depth - 3, 1)

    halo0("h0", "k0", 3, 6, True, 5)
    halo0("h0", "f0", 2, 4, True, 4)

    def put1(group, name, which):
        ref = B[name]
        for dz, dy in which:
            if (dz, dy) in knights:
                sq, tq, lq = nearest(dz, 1, 2)
                sy, ty, ly = nearest(dy, 2, 4)
            else:
                sq, tq, lq = 0, -2 * dz, 2
                sy, ty, ly = 0, -4 * dy, 4
            put(group, ref.at[pl.ds(sq + 4, lq), pl.ds(sy + 8, ly)], ref.at[pl.ds(tq + 4, lq), pl.ds(ty + 8, ly)], lq * ly, dz, dy)

    def coarse1(read, target):
        def body(y1, c):
            even = (lane // 2 + y1) & 1 == 0
            cols = []
            for z1 in range(4):
                t = read(z1, 2 * y1) + read(z1, 2 * y1 + 1)
                cols.append((t + pltpu.roll(t, 127, 1)) * 0.125)
            for q in range(2):
                lo, hi = cols[2 * q], cols[2 * q + 1]
                red, black = jnp.where(even, lo, hi), jnp.where(even, hi, lo)
                target[q + 4, y1 + 8] = jnp.where(lane % 2 == 0, red, pltpu.roll(black, 1, 1))
            return c

        lax.fori_loop(0, 4, body, 0)

    def coarse2(read):
        out = jnp.zeros(T8, F32)
        for y2 in range(2):
            for z2 in range(2):
                t = read(z2, 2 * y2) + read(z2, 2 * y2 + 1)
                t = (t + pltpu.roll(t, 126, 1)) * 0.125
                for j in range(2):
                    v = jnp.take_along_axis(t, (lane % 16) * 8 + 4 * j, axis=1)
                    v = jnp.sum(jnp.where(lane // 16 == sub, v, 0.0), axis=0, keepdims=True)
                    out = jnp.where(sub == y2 * 4 + z2 * 2 + j, jnp.broadcast_to(v, T8), out)
        return out

    k0, c1k, c1f = B["k0"], B["c1k"], B["c1f"]
    coarse1(lambda z, y: k0[0, z + 3, y + 6] + k0[1, z + 3, y + 6], c1k)
    put1("k1", "c1k", ring + far + knights)
    m2k, m2f = B["m2k"], B["m2f"]

    def both1(q, y):
        v = c1k[q + 4, y + 8]
        return v + pltpu.roll(v, 127, 1)

    m2k[4, gz] = coarse2(both1)
    for dz, dy in patch:
        put("k2", m2k.at[4, gz], m2k.at[4 - dy, gz], 1, dz, dy)

    def shifts(v, st, edge):
        a = pltpu.roll(v, st, 1)
        m = jnp.where(lane < st, pltpu.roll(a, 1, 0), a)
        a = pltpu.roll(v, 128 - st, 1)
        p = jnp.where(lane >= 128 - st, pltpu.roll(a, 7, 0), a)
        if edge:
            m = jnp.where((lane < st) & (sub == 0), 0.0, m)
            p = jnp.where((lane >= 128 - st) & (sub == 7), 0.0, p)
        return m, p

    def row_neighbours(ref, qs, y, colour, st, edge):
        at = {q: ref[q, y] for q in range(qs[0] - 1, qs[-1] + 2)}
        low = (lane // st + y + colour) & 1 == 0
        out = []
        for q in qs:
            o = at[q]
            m, p = shifts(o, st, edge)
            out.append((o, jnp.where(low, at[q - 1], at[q + 1]), ref[q, y - 1], ref[q, y + 1], m, p))
        return out

    def weights(own, others):
        diag = 0.5 * (6.0 * own + sum(others[1:], others[0]))
        inverse = jnp.where(own > 0.0, 1.0 / diag, 0.0)
        return inverse, [jnp.where(k > 0.0, 0.5 * (own + k) * inverse, 0.0) for k in others]

    def weigh(level, colour, oq, oy, wq, wy, q0, q1, y0, y1, st):
        k, w, d = B["k%d" % level], B["w%d" % level], B["d%d" % level]

        def body(y, c):
            qs = [q + oq for q in range(q0, q1 + 1)]
            near = row_neighbours(k.at[1 - colour], qs, y + oy, colour, st, True)
            for q, others in zip(qs, near):
                inverse, ws = weights(k[colour, q, y + oy], others)
                d[colour, q - oq + wq, y + wy] = inverse
                for i in range(6):
                    w[colour, i, q - oq + wq, y + wy] = ws[i]
            return c

        loop(y0, y1 + 1, body)

    def fresh(level, colour, qs, y, other, oq, oy, wq, wy, st):
        w, g = B["w%d" % level], B["g%d" % level]
        near = row_neighbours(other, [q + oq for q in qs], y + oy, colour, st, False)
        out = []
        for q, u in zip(qs, near):
            at = (q + wq, y + wy)
            acc = g[(colour,) + at]
            for i in range(6):
                acc = acc + w[(colour, i) + at] * u[i]
            out.append(acc)
        return out

    def half_sweep(level, colour, target, other, q0, q1, y0, y1):
        oq, oy, wq, wy, st = PLACE[level]

        def body(y, c):
            qs = list(range(q0, q1 + 1))
            for q, v in zip(qs, fresh(level, colour, qs, y, other, oq, oy, wq, wy, st)):
                target[q + oq, y + oy] = v
            return c

        loop(y0, y1 + 1, body)

    def residual(level, colour, own, other, qs, y):
        oq, oy, wq, wy, st = PLACE[level]
        d = B["d%d" % level]
        new = fresh(level, colour, qs, y, other, oq, oy, wq, wy, st)
        return [(v - own[q + oq, y + oy]) / (d[colour, q + wq, y + wy] * 4.0**level) for q, v in zip(qs, new)]

    PLACE = {0: (3, 6, 2, 4, 1), 1: (4, 8, 3, 6, 2)}

    received("h0")

    def blank(name, at):
        ref = B[name]
        shape = BUFFERS[name]
        size = [len(range(*a.indices(n))) if isinstance(a, slice) else None for a, n in zip(at, shape)]
        ref[at] = jnp.zeros(tuple(s for s in size if s is not None) + T8, F32)

    ALL = slice(None)
    for side, cut in ((gz == 0, (ALL, slice(0, 3))), (gz == nz - 1, (ALL, slice(7, 10))),
                      (gy == 0, (ALL, ALL, slice(0, 6))), (gy == ny - 1, (ALL, ALL, slice(14, 20)))):
        @pl.when(side)
        def _(cut=cut):
            for colour in range(2):
                if len(cut) == 2:
                    for q in range(cut[1].start, cut[1].stop):
                        blank("k0", (colour, q, slice(0, 20)))
                else:
                    for q in range(10):
                        blank("k0", (colour, q, cut[2]))

    weigh(0, 0, 3, 6, 2, 4, -2, 5, -4, 11, 1)
    weigh(0, 1, 3, 6, 2, 4, -2, 5, -3, 10, 1)
    f0, d0, g0, r0, b0, p0, s0 = (B[n] for n in ("f0", "d0", "g0", "r0", "b0", "p0", "s0"))

    def start0(y, c):
        for q in range(8):
            red = f0[0, q, y] * d0[0, q, y]
            g0[0, q, y] = red
            r0[q + 1, y + 2] = red
        return c

    lax.fori_loop(0, 16, start0, 0)

    def start0b(y, c):
        for q in range(8):
            g0[1, q, y] = f0[1, q, y] * d0[1, q, y]
        return c

    lax.fori_loop(1, 15, start0b, 0)
    half_sweep(0, 1, b0, r0, -2, 5, -3, 10)
    half_sweep(0, 0, r0, b0, -1, 4, -2, 9)
    half_sweep(0, 1, b0, r0, -1, 4, -1, 8)

    def rest0(y, c):
        qs = list(range(4))
        red = residual(0, 0, r0, b0, qs, y)
        black = residual(0, 1, b0, r0, qs, y)
        for q in qs:
            s0[q, y] = red[q] + black[q]
            p0[q + 3, y + 6] = b0[q + 3, y + 6]
        return c

    lax.fori_loop(0, 8, rest0, 0)
    coarse1(lambda z, y: s0[z, y], c1f)
    put1("f1", "c1f", ring)
    put1("f1x", "c1f", far + knights)
    halo0("u0", "p0", 3, 6, False, 5)

    received("k1")
    k1 = B["k1"]
    for side, q_cut, y_cut in ((gz == 0, (0, 4), None), (gz == 1, (0, 2), None), (gz == nz - 1, (6, 10), None), (gz == nz - 2, (8, 10), None),
                               (gy == 0, None, (0, 8)), (gy == 1, None, (0, 4)), (gy == ny - 1, None, (12, 20)), (gy == ny - 2, None, (16, 20))):
        @pl.when(side)
        def _(q_cut=q_cut, y_cut=y_cut):
            for q in range(*(q_cut or (0, 10))):
                blank("c1k", (q, slice(*(y_cut or (0, 20)))))

    def open1(y, c):
        for q in range(10):
            v = c1k[q, y]
            k1[0, q, y] = v
            k1[1, q, y] = pltpu.roll(v, 127, 1)
        return c

    lax.fori_loop(0, 20, open1, 0)
    weigh(1, 0, 4, 8, 3, 6, -3, 4, -6, 9, 2)
    weigh(1, 1, 4, 8, 3, 6, -3, 4, -5, 8, 2)

    received("k2")
    k2, w2, d2, g2, r2, b2, p2 = (B[n] for n in ("k2", "w2", "d2", "g2", "r2", "b2", "p2"))

    def open2(ref, d, y2, zp, j):
        return ref.reshape(576, 128)[pl.ds(d * 64 + y2 * 4 + zp * 2 + j, 8, stride=8), :]

    def fill2(d, c):
        there = gy + d - 4
        inside = jnp.where((there >= 0) & (there < ny), 1.0, 0.0)
        for y2 in range(2):
            for zp in range(2):
                for colour in range(2):
                    k2[colour, 2 * d + y2 + 1, zp] = open2(m2k, d, y2, zp, (colour + y2 + zp) % 2) * inside
        return c

    lax.fori_loop(0, 9, fill2, 0)

    def near2(ref, row, p, zp, colour, edge):
        o, oz = ref[row, zp], ref[row, 1 - zp]
        if (colour + p + zp) % 2 == 0:
            x = pltpu.roll(o, 1, 1)
            x = jnp.where(lane == 0, 0.0, x) if edge else x
        else:
            x = pltpu.roll(o, 127, 1)
            x = jnp.where(lane == 127, 0.0, x) if edge else x
        if zp == 0:
            z = pltpu.roll(oz, 1, 0)
            z = jnp.where(sub == 0, 0.0, z) if edge else z
        else:
            z = pltpu.roll(oz, 7, 0)
            z = jnp.where(sub == 7, 0.0, z) if edge else z
        return (oz, z, ref[row - 1, zp], ref[row + 1, zp], o, x)

    def weigh2(d, c):
        for p in range(2):
            for zp in range(2):
                for colour in range(2):
                    row = 2 * d + p
                    inverse, ws = weights(k2[colour, row + 1, zp], near2(k2.at[1 - colour], row + 1, p, zp, colour, True))
                    d2[colour, row, zp] = inverse
                    for i in range(6):
                        w2[colour, i, row, zp] = ws[i]
        return c

    lax.fori_loop(0, 9, weigh2, 0)

    def fresh2(d, p, zp, colour, other):
        row = 2 * d + p
        u = near2(other, row + 1, p, zp, colour, False)
        acc = g2[colour, row, zp]
        for i in range(6):
            acc = acc + w2[colour, i, row, zp] * u[i]
        return acc

    def half_sweep2(colour, target, other, d0_, d1_):
        def body(d, c):
            for p in range(2):
                for zp in range(2):
                    target[2 * d + p + 1, zp] = fresh2(d, p, zp, colour, other)
            return c

        lax.fori_loop(d0_, d1_ + 1, body, 0)

    m3k, m3f = B["m3k"], B["m3f"]
    total = jnp.zeros(T8, F32)
    for p in range(2):
        for zp in range(2):
            for colour in range(2):
                total = total + k2[colour, 9 + p, zp]
    m3k[gy] = total * 0.125
    for dy in line:
        put("k3", m3k.at[gy], m3k.at[gy], 1, 0, dy)

    received("f1")
    d1, g1, r1, b1, p1, s1 = (B[n] for n in ("d1", "g1", "r1", "b1", "p1", "s1"))

    def start1(q0, q1, y0, y1, write):
        def body(y, c):
            for q in range(q0, q1 + 1):
                v = c1f[q + 4, y + 8]
                red = v * (4.0 * d1[0, q + 3, y + 6])
                g1[0, q + 3, y + 6] = red
                if write:
                    r1[q + 4, y + 8] = red
                g1[1, q + 3, y + 6] = pltpu.roll(v, 127, 1) * (4.0 * d1[1, q + 3, y + 6])
            return c

        loop(y0, y1 + 1, body)

    start1(-2, 3, -4, 7, True)
    half_sweep(1, 1, b1, r1, -2, 3, -3, 6)
    half_sweep(1, 0, r1, b1, -1, 2, -2, 5)
    half_sweep(1, 1, b1, r1, -1, 2, -1, 4)

    def rest1(y, c):
        qs = [0, 1]
        red = residual(1, 0, r1, b1, qs, y)
        black = residual(1, 1, b1, r1, qs, y)
        for q in qs:
            s1[q, y] = red[q] + black[q]
            p1[q + 4, y + 8] = b1[q + 4, y + 8]
        return c

    lax.fori_loop(0, 4, rest1, 0)
    m2f[4, gz] = coarse2(lambda q, y: s1[q, y])
    for dz, dy in patch:
        if abs(dy) <= 2:
            put("f2", m2f.at[4, gz], m2f.at[4 - dy, gz], 1, dz, dy)
    put1("u1", "p1", ring + far + knights)

    received("k3")
    k3, w3, d3, g3, r3, b3, e3 = (B[n] for n in ("k3", "w3", "d3", "g3", "r3", "b3", "e3"))
    even3 = (lane + sub) % 2 == 0
    for m in range(16):
        lo, hi = m3k[2 * m], m3k[2 * m + 1]
        k3[0, m + 1] = jnp.where(even3, lo, hi)
        k3[1, m + 1] = jnp.where(even3, hi, lo)

    def near3(ref, m, colour, edge):
        o = ref[m + 1]
        low = even3 if colour == 0 else jnp.logical_not(even3)
        zm, zp, xm, xp = pltpu.roll(o, 1, 0), pltpu.roll(o, 7, 0), pltpu.roll(o, 1, 1), pltpu.roll(o, 127, 1)
        if edge:
            zm, zp = jnp.where(sub == 0, 0.0, zm), jnp.where(sub == 7, 0.0, zp)
            xm, xp = jnp.where(lane == 0, 0.0, xm), jnp.where(lane == 127, 0.0, xp)
        return (o, jnp.where(low, ref[m], ref[m + 2]), zm, zp, xm, xp)

    def weigh3(m, c):
        for colour in range(2):
            inverse, ws = weights(k3[colour, m + 1], near3(k3.at[1 - colour], m, colour, True))
            d3[colour, m] = inverse * 64.0
            for i in range(6):
                w3[colour, i, m] = ws[i]
        return c

    lax.fori_loop(0, 16, weigh3, 0)

    received("f2")

    def start2(d0_, d1_, write):
        def body(d, c):
            for y2 in range(2):
                for zp in range(2):
                    for colour in range(2):
                        row = 2 * d + y2
                        v = open2(m2f, d, y2, zp, (colour + y2 + zp) % 2) * (16.0 * d2[colour, row, zp])
                        g2[colour, row, zp] = v
                        if write and colour == 0:
                            r2[row + 1, zp] = v
            return c

        lax.fori_loop(d0_, d1_ + 1, body, 0)

    start2(2, 6, True)
    half_sweep2(1, b2, r2, 2, 6)
    half_sweep2(0, r2, b2, 3, 5)
    half_sweep2(1, b2, r2, 3, 5)
    total = jnp.zeros(T8, F32)
    for p in range(2):
        for zp in range(2):
            for colour in range(2):
                own, other = (r2, b2) if colour == 0 else (b2, r2)
                v = fresh2(4, p, zp, colour, other) - own[9 + p, zp]
                total = total + v / (d2[colour, 8 + p, zp] * 16.0)
            p2[9 + p, zp] = b2[9 + p, zp]
    m3f[gy] = total * 0.125
    for dy in line:
        put("f3", m3f.at[gy], m3f.at[gy], 1, 0, dy)
    for dz, dy in patch:
        if abs(dy) > 2:
            put("f2x", m2f.at[4, gz], m2f.at[4 - dy, gz], 1, dz, dy)
    for dy in range(-4, 5):
        if dy:
            put("u2", p2.at[pl.ds(9, 2)], p2.at[pl.ds(9 - 2 * dy, 2)], 4, 0, dy)

    received("f1x")
    start1(-3, 4, -6, 9, False)

    received("f3")
    for m in range(16):
        lo, hi = m3f[2 * m], m3f[2 * m + 1]
        red = jnp.where(even3, lo, hi) * d3[0, m]
        g3[0, m] = red
        r3[m + 1] = red
        g3[1, m] = jnp.where(even3, hi, lo) * d3[1, m]

    def half_sweep3(colour, target, other):
        for m in range(16):
            u = near3(other, m, colour, False)
            acc = g3[colour, m]
            for i in range(6):
                acc = acc + w3[colour, i, m] * u[i]
            target[m + 1] = acc

    half_sweep3(1, b3, r3)

    def sweep3(s, c):
        half_sweep3(0, r3, b3)
        half_sweep3(1, b3, r3)
        return c

    lax.fori_loop(0, 11, sweep3, 0)
    for m in range(16):
        red, black = r3[m + 1], b3[m + 1]
        e3[2 * m + 4] = jnp.where(even3, red, black)
        e3[2 * m + 5] = jnp.where(even3, black, red)

    received("f2x")
    start2(0, 1, False)
    start2(7, 8, False)
    received("u2")
    finished("u2")

    def up2(d, c):
        e = e3[gy + d]
        for p in range(2):
            for zp in range(2):
                p2[2 * d + p + 1, zp] = p2[2 * d + p + 1, zp] + e
        return c

    lax.fori_loop(0, 9, up2, 0)
    half_sweep2(0, r2, p2, 0, 8)
    half_sweep2(1, p2, r2, 1, 7)
    half_sweep2(0, r2, p2, 1, 7)
    half_sweep2(1, p2, r2, 2, 6)

    e2v, e2x = B["e2v"], B["e2x"]

    def store2(d, c):
        for p in range(2):
            for zp in range(2):
                for colour in range(2):
                    ref = r2 if colour == 0 else p2
                    e2v[2 * (d - 2) + p, zp, (colour + p + zp) % 2, pl.ds(8, 8), :] = ref[2 * d + p + 1, zp]
        return c

    lax.fori_loop(2, 7, store2, 0)
    spread = 16 * sub + lane // 8

    def spread2(y2, c):
        for z2 in range(-4, 6):
            parts = []
            for j in range(2):
                row = e2v[y2, z2 % 2, j, pl.ds(8 + gz + z2 // 2, 1), :]
                parts.append(jnp.take_along_axis(jnp.broadcast_to(row, T8), spread, axis=1))
            e2x[z2 + 4, y2] = jnp.where((lane // 4) % 2 == 0, parts[0], parts[1])
        return c

    lax.fori_loop(0, 10, spread2, 0)

    received("u1")
    finished("u1")

    def up1(y2, c):
        for q in range(10):
            e = e2x[q, y2]
            for p in range(2):
                p1[q, 2 * y2 + p] = p1[q, 2 * y2 + p] + e
        return c

    lax.fori_loop(0, 10, up1, 0)
    half_sweep(1, 0, r1, p1, -3, 4, -6, 9)
    half_sweep(1, 1, p1, r1, -3, 4, -5, 8)
    half_sweep(1, 0, r1, p1, -2, 3, -4, 7)
    half_sweep(1, 1, p1, r1, -2, 3, -3, 6)

    received("u0")
    finished("u0")

    def up0(y1, c):
        even = (lane // 2 + y1) & 1 == 0
        for q in range(-2, 4):
            red, black = r1[q + 4, y1 + 8], p1[q + 4, y1 + 8]
            for p in range(2):
                z1 = 2 * q + p
                if -3 <= z1 <= 6:
                    e = jnp.where(even, red, black) if p == 0 else jnp.where(even, black, red)
                    e = jnp.where(lane % 2 == 0, e, pltpu.roll(e, 1, 1))
                    for i in range(2):
                        p0[z1 + 3, 2 * y1 + i + 6] = p0[z1 + 3, 2 * y1 + i + 6] + e
        return c

    loop(-3, 7, up0)
    half_sweep(0, 0, r0, p0, -2, 5, -4, 11)
    half_sweep(0, 1, p0, r0, -2, 5, -3, 10)
    half_sweep(0, 0, r0, p0, -1, 4, -2, 9)
    half_sweep(0, 1, p0, r0, -1, 4, -1, 8)

    out_u, out_r = B["stage_f"].reshape(512, 128), B["stage_k"].reshape(512, 128)

    def finish(y, c):
        even = (lane + y) & 1 == 0
        qs = list(range(4))
        res_red = residual(0, 0, r0, p0, qs, y)
        res_black = residual(0, 1, p0, r0, qs, y)
        for q in qs:
            red, black = r0[q + 3, y + 6], p0[q + 3, y + 6]
            lo, hi = pl.ds(2 * q * 64 + y, 8, stride=8), pl.ds((2 * q + 1) * 64 + y, 8, stride=8)
            out_u[lo, :] = jnp.where(even, red, black)
            out_u[hi, :] = jnp.where(even, black, red)
            out_r[lo, :] = jnp.where(even, res_red[q], res_black[q])
            out_r[hi, :] = jnp.where(even, res_black[q], res_red[q])
        return c

    lax.fori_loop(0, 8, finish, 0)
    for c in pieces(u_out, B["stage_f"], in_sem.at[0], True) + pieces(r_out, B["stage_k"], in_sem.at[1], True):
        c.start()
    for group in GROUPS:
        if group not in ("u0", "u1", "u2"):
            finished(group)
    wait_bytes(in_sem.at[0], 64)
    wait_bytes(in_sem.at[1], 64)


def solution(mesh):
    nz, ny = mesh.shape["gz"], mesh.shape["gy"]

    def on_device(right_side, coefficient):
        out = jax.ShapeDtypeStruct(right_side.shape, F32)

        def body(*refs):
            kernel(nz, ny, *refs)

        scratch = []
        for name, shape in BUFFERS.items():
            if name in ("stage_f", "stage_k"):
                scratch.append(pltpu.VMEM((8, 8, 8, 128), F32))
            elif name == "e2v":
                scratch.append(pltpu.VMEM((10, 2, 2, 24, 128), F32))
            else:
                scratch.append(pltpu.VMEM(shape + T8, F32))
        return pl.pallas_call(
            body,
            out_shape=(out, out),
            in_specs=[pl.BlockSpec(memory_space=pl.ANY)] * 2,
            out_specs=[pl.BlockSpec(memory_space=pl.ANY)] * 2,
            scratch_shapes=scratch
            + [pltpu.SemaphoreType.DMA((2,)), pltpu.SemaphoreType.DMA((len(GROUPS),)), pltpu.SemaphoreType.DMA((len(GROUPS),))],
            compiler_params=pltpu.CompilerParams(collective_id=0, has_side_effects=True, vmem_limit_bytes=56 * 1024 * 1024),
            name="vcycle",
        )(right_side, coefficient)

    placed = (P("gz", "gy", None), P("gz", "gy", None))
    return jax.shard_map(on_device, mesh=mesh, in_specs=placed, out_specs=placed, check_vma=False)
```

time: 827 us -> 83.7 us (0.10)
  the two profiles are of different devices: /device:TPU:103 before, /device:TPU:1 now
where the time goes in v1:
time: 83.7 us; the launch traced here: 83.3 us
  Pallas kernels  80.3 us (96%)
  local copies, waits for them, and re-layouts  2.42 us (3%)
    pallas_call x1, Pallas kernels, on_device(): pl.pallas_call(body, out_shape=(out, out), in_specs=[pl.BlockSpec(memory_...  80.3 us
    unnamed x4, local copies, waits for them, and re-layouts  2.42 us

profile of v1, /device:TPU:1, one launch (start us, length us, event | category | flops | bytes accessed | tf_op | source)
XLA Modules:
  0.0 83.3 jit_solution(6290358921946955110)
XLA Ops:
  0.6 80.3 %vcycle.1 = (f32[8,8,1024]{2,1,0:T(8,128)}, f32[8,8,1024]{2,1,0:T(8,128)}) custom-call(f32[8,8,1024]{2,1,0:T(8,128)} %refs_0_.1, f32[8,8,1024]{2,1,0:T(8,128)} %refs_1_.1), custom_call_target="tpu_custom_call" | custom-call | tf_op jit(solution)/shard_map/vcycle/pallas_call | solution.py:692
  80.9 0.0 copy-start
  80.9 1.7 %copy.6 = f32[8,8,1024]{2,1,0:T(8,128)} copy(f32[8,8,1024]{2,1,0:T(8,128)} %get-tuple-element.4) | data formatting | bytes 524288
  82.6 0.0 copy-done
  82.6 0.7 copy.7
Async XLA Ops:
  80.9 1.7 %copy-start = (f32[8,8,1024]{2,1,0:T(8,128)S(1)}, f32[8,8,1024]{2,1,0:T(8,128)}, u32[]{:S(2)}) copy-start(f32[8,8,1024]{2,1,0:T(8,128)} %get-tuple-element.5) | copy-start | bytes 786436

commit v2 on v1

--- a/solution.py
+++ b/solution.py
@@ -19,8 +19,7 @@
     e2v=(10, 2, 2, 3), e2x=(10, 10),
     m3k=(32,), m3f=(32,), k3=(2, 18), w3=(2, 6, 16), d3=(2, 16), g3=(2, 16), r3=(18,), b3=(18,), e3=(40,),
 )
-ZEROED = ("k0", "f0", "r0", "b0", "p0", "c1k", "c1f", "r1", "b1", "p1", "k2", "r2", "b2", "p2", "e2v", "k3", "r3", "b3", "e3")
-GROUPS = ("h0", "k1", "k2", "f1", "f1x", "u0", "u1", "k3", "f2", "f2x", "u2", "f3")
+GROUPS = ("h0", "k1", "k2", "k2x", "f1", "f1x", "u0", "u1", "k3", "f2", "f2x", "u2", "f3")
 
 
 def iota(dim):
@@ -35,12 +34,17 @@
     return 0, -d * size, n
 
 
-def loop(first, end, body):
+def loop(first, end, body, rows=2):
+    steps = (end - first) // rows
+
     def shifted(i, c):
-        body(i - 8, c)
-        return c
-
-    lax.fori_loop(first + 8, end + 8, shifted, 0)
+        for n in range(rows):
+            body(i * rows + (first + n), c)
+        return c
+
+    lax.fori_loop(0, steps, shifted, 0)
+    for y in range(first + steps * rows, end):
+        body(jnp.int32(y), 0)
 
 
 def kernel(nz, ny, f_in, k_in, u_out, r_out, *scratch):
@@ -67,30 +71,12 @@
     for c in pieces(k_in, B["stage_k"], in_sem.at[0], False) + pieces(f_in, B["stage_f"], in_sem.at[1], False):
         c.start()
 
-    for name in ZEROED:
-        shape = BUFFERS[name]
-        ref = B[name]
-        if len(shape) == 3 and shape[0] == 2:
-            for i in range(2):
-                def clear2(j, c, ref=ref, i=i, shape=shape):
-                    ref[i, j] = jnp.zeros(shape[2:] + T8, F32)
-                    return c
-                lax.fori_loop(0, shape[1], clear2, 0)
-        else:
-            def clear(j, c, ref=ref, shape=shape):
-                if shape[-1] == 3:
-                    ref[j] = jnp.zeros((2, 2, 24, 128), F32)
-                else:
-                    ref[j] = jnp.zeros(shape[1:] + T8, F32)
-                return c
-            lax.fori_loop(0, shape[0], clear, 0)
-
-    ring = [(a, b) for a in (-1, 0, 1) for b in (-1, 0, 1) if (a, b) != (0, 0)]
+    ring = [(0, 1), (0, -1), (1, 1), (1, -1), (-1, 1), (-1, -1), (1, 0), (-1, 0)]
     far = [(2, 0), (-2, 0), (0, 2), (0, -2)]
     knights = [(a, b) for a in (-2, -1, 1, 2) for b in (-2, -1, 1, 2) if abs(a) != abs(b)]
-    patch = [(a, b) for b in range(-4, 5) for a in range(nz) if (a, b) != (0, 0)]
-    line = [b for b in range(1, ny)]
-    everyone = patch + [(0, b) for b in line if 4 < b < ny - 4]
+    patch = [(a, b) for b in (2, -2, 1, -1, 0) for a in range(nz) if (a, b) != (0, 0)]
+    line = sorted(range(1, ny), key=lambda b: -min(b, ny - b))
+    everyone = patch + [(0, b) for b in line if 2 < b < ny - 2]
     barrier = pltpu.get_barrier_semaphore()
     for dz, dy in everyone:
         pl.semaphore_signal(barrier, inc=1, device_id=device(dz, dy), device_id_type=MESH)
@@ -122,7 +108,7 @@
                 target[1, q + oq, y + oy] = jnp.where(even, hi, lo)
             return c
 
-        lax.fori_loop(0, 8, body, 0)
+        loop(0, 8, body)
 
     wait_bytes(in_sem.at[0], 64)
     packed("stage_k", "k0", 3, 6)
@@ -130,32 +116,47 @@
     packed("stage_f", "f0", 2, 4)
     pl.semaphore_wait(barrier, len(everyone))
 
-    def put0(group, name, oq, oy, colours, dz, dy, nq, nyy, skip_q=0):
+    covered = {}
+
+    def put0(group, name, oq, oy, colour, dz, dy, nq, nyy, skip_q=0):
         sq, tq, lq = nearest(dz, nq, 4)
         sy, ty, ly = nearest(dy, nyy, 8)
         if skip_q:
             lq = nq - skip_q
             if dz < 0:
                 sq, tq = sq + skip_q, tq + skip_q
-        ref = B[name]
-        src, dst = (
-            (pl.ds(sq + oq, lq), pl.ds(sy + oy, ly)),
-            (pl.ds(tq + oq, lq), pl.ds(ty + oy, ly)),
-        )
-        if colours:
-            put(group, ref.at[(slice(None),) + src], ref.at[(slice(None),) + dst], 2 * lq * ly, dz, dy)
-        else:
-            put(group, ref.at[src], ref.at[dst], lq * ly, dz, dy)
-
-    def halo0(group, name, oq, oy, colours, depth):
-        for dz, dy in ((0, 1), (0, -1), (1, 0), (-1, 0)):
-            put0(group, name, oq, oy, colours, dz, dy, (depth + 1) // 2, depth)
+        if lq <= 0 or ly <= 0:
+            return
+        ref = B[name] if colour is None else B[name].at[colour]
+        covered.setdefault((name, colour), set()).update((tq + i + oq, ty + j + oy) for i in range(lq) for j in range(ly))
+        put(group, ref.at[pl.ds(sq + oq, lq), pl.ds(sy + oy, ly)], ref.at[pl.ds(tq + oq, lq), pl.ds(ty + oy, ly)], lq * ly, dz, dy)
+
+    def halo0(group, fields):
+        for dz, dy in ((0, 1), (0, -1)):
+            for name, oq, oy, colour, depth in fields:
+                put0(group, name, oq, oy, colour, dz, dy, 0, depth)
         for dz, dy in ((1, 1), (1, -1), (-1, 1), (-1, -1)):
-            put0(group, name, oq, oy, colours, dz, dy, 1, depth - 1)
-            put0(group, name, oq, oy, colours, dz, dy, 2, depth - 3, 1)
-
-    halo0("h0", "k0", 3, 6, True, 5)
-    halo0("h0", "f0", 2, 4, True, 4)
+            for name, oq, oy, colour, depth in fields:
+                put0(group, name, oq, oy, colour, dz, dy, 1, depth - 1)
+                put0(group, name, oq, oy, colour, dz, dy, 2, depth - 3, 1)
+        for dz, dy in ((1, 0), (-1, 0)):
+            for name, oq, oy, colour, depth in fields:
+                put0(group, name, oq, oy, colour, dz, dy, (depth + 1) // 2, 0)
+
+    halo0("h0", [("k0", 3, 6, 1, 5), ("k0", 3, 6, 0, 4), ("f0", 2, 4, 0, 4), ("f0", 2, 4, 1, 3)])
+
+    def clear(name, index, own, got):
+        nq, nyy = BUFFERS[name][-2:]
+        have = got | {(own[0] + i, own[1] + j) for i in range(own[2]) for j in range(own[3])}
+        for q in range(nq):
+            y = 0
+            while y < nyy:
+                end = y
+                while end < nyy and (q, end) not in have:
+                    end += 1
+                if end > y:
+                    B[name][index + (q, slice(y, end))] = jnp.zeros((end - y,) + T8, F32)
+                y = end + 1
 
     def put1(group, name, which):
         ref = B[name]
@@ -166,6 +167,7 @@
             else:
                 sq, tq, lq = 0, -2 * dz, 2
                 sy, ty, ly = 0, -4 * dy, 4
+            covered.setdefault((name, None), set()).update((tq + i + 4, ty + j + 8) for i in range(lq) for j in range(ly))
             put(group, ref.at[pl.ds(sq + 4, lq), pl.ds(sy + 8, ly)], ref.at[pl.ds(tq + 4, lq), pl.ds(ty + 8, ly)], lq * ly, dz, dy)
 
     def coarse1(read, target):
@@ -181,7 +183,7 @@
                 target[q + 4, y1 + 8] = jnp.where(lane % 2 == 0, red, pltpu.roll(black, 1, 1))
             return c
 
-        lax.fori_loop(0, 4, body, 0)
+        loop(0, 4, body)
 
     def coarse2(read):
         out = jnp.zeros(T8, F32)
@@ -205,8 +207,51 @@
         return v + pltpu.roll(v, 127, 1)
 
     m2k[4, gz] = coarse2(both1)
-    for dz, dy in patch:
-        put("k2", m2k.at[4, gz], m2k.at[4 - dy, gz], 1, dz, dy)
+    for dz in range(1, nz):
+        put("k2", m2k.at[4, gz], m2k.at[4, gz], 1, dz, 0)
+
+    own0, own1 = (3, 6, 4, 8), (4, 8, 2, 4)
+    for colour in range(2):
+        clear("k0", (colour,), own0, covered["k0", colour])
+        clear("f0", (colour,), (2, 4, 4, 8), covered["f0", colour])
+    clear("p0", (), own0, covered["k0", 1])
+    for name in ("c1k", "c1f", "p1"):
+        clear(name, (), own1, covered["c1k", None])
+
+    def wipe(i, c):
+        for name in ("r0", "b0", "r1", "b1"):
+            B[name][i] = jnp.zeros((20,) + T8, F32)
+        B["e2v"][i] = jnp.zeros((2, 2, 24, 128), F32)
+        return c
+
+    lax.fori_loop(0, 10, wipe, 0)
+    for row in (0, 19):
+        for colour in range(2):
+            B["k2"][colour, row] = jnp.zeros((2,) + T8, F32)
+        B["p2"][row] = jnp.zeros((2,) + T8, F32)
+    for name in ("r2", "b2"):
+        B[name][...] = jnp.zeros((20, 2) + T8, F32)
+    for m in (0, 17):
+        for colour in range(2):
+            B["k3"][colour, m] = jnp.zeros(T8, F32)
+        B["r3"][m] = jnp.zeros(T8, F32)
+        B["b3"][m] = jnp.zeros(T8, F32)
+    for m in (0, 36):
+        B["e3"][m:m + 4] = jnp.zeros((4,) + T8, F32)
+
+    def open2(ref, d, y2, zp, j):
+        return ref.reshape(576, 128)[pl.ds(d * 64 + y2 * 4 + zp * 2 + j, 8, stride=8), :]
+
+    received("k2")
+    total = jnp.zeros(T8, F32)
+    for n in range(8):
+        total = total + open2(m2k, 4, n // 4, n // 2 % 2, n % 2)
+    m3k, m3f = B["m3k"], B["m3f"]
+    m3k[gy] = total * 0.125
+    for dy in (4, -4, 3, -3, 2, -2, 1, -1):
+        put("k2x", m2k.at[4], m2k.at[4 - dy], 8, 0, dy)
+    for dy in line:
+        put("k3", m3k.at[gy], m3k.at[gy], 1, 0, dy)
 
     def shifts(v, st, edge):
         a = pltpu.roll(v, st, 1)
@@ -263,13 +308,17 @@
     def half_sweep(level, colour, target, other, q0, q1, y0, y1):
         oq, oy, wq, wy, st = PLACE[level]
 
-        def body(y, c):
-            qs = list(range(q0, q1 + 1))
-            for q, v in zip(qs, fresh(level, colour, qs, y, other, oq, oy, wq, wy, st)):
-                target[q + oq, y + oy] = v
+        qs = list(range(q0, q1 + 1))
+
+        def body(i, c):
+            rows = [2 * i + y0, 2 * i + y0 + 1]
+            values = [fresh(level, colour, qs, y, other, oq, oy, wq, wy, st) for y in rows]
+            for y, row in zip(rows, values):
+                for q, v in zip(qs, row):
+                    target[q + oq, y + oy] = v
             return c
 
-        loop(y0, y1 + 1, body)
+        lax.fori_loop(0, (y1 + 1 - y0) // 2, body, 0)
 
     def residual(level, colour, own, other, qs, y):
         oq, oy, wq, wy, st = PLACE[level]
@@ -311,14 +360,14 @@
             r0[q + 1, y + 2] = red
         return c
 
-    lax.fori_loop(0, 16, start0, 0)
+    loop(0, 16, start0)
 
     def start0b(y, c):
         for q in range(8):
             g0[1, q, y] = f0[1, q, y] * d0[1, q, y]
         return c
 
-    lax.fori_loop(1, 15, start0b, 0)
+    loop(1, 15, start0b)
     half_sweep(0, 1, b0, r0, -2, 5, -3, 10)
     half_sweep(0, 0, r0, b0, -1, 4, -2, 9)
     half_sweep(0, 1, b0, r0, -1, 4, -1, 8)
@@ -332,11 +381,11 @@
             p0[q + 3, y + 6] = b0[q + 3, y + 6]
         return c
 
-    lax.fori_loop(0, 8, rest0, 0)
+    loop(0, 8, rest0)
     coarse1(lambda z, y: s0[z, y], c1f)
     put1("f1", "c1f", ring)
     put1("f1x", "c1f", far + knights)
-    halo0("u0", "p0", 3, 6, False, 5)
+    halo0("u0", [("p0", 3, 6, None, 5)])
 
     received("k1")
     k1 = B["k1"]
@@ -354,15 +403,12 @@
             k1[1, q, y] = pltpu.roll(v, 127, 1)
         return c
 
-    lax.fori_loop(0, 20, open1, 0)
+    loop(0, 20, open1)
     weigh(1, 0, 4, 8, 3, 6, -3, 4, -6, 9, 2)
     weigh(1, 1, 4, 8, 3, 6, -3, 4, -5, 8, 2)
 
-    received("k2")
+    received("k2x")
     k2, w2, d2, g2, r2, b2, p2 = (B[n] for n in ("k2", "w2", "d2", "g2", "r2", "b2", "p2"))
-
-    def open2(ref, d, y2, zp, j):
-        return ref.reshape(576, 128)[pl.ds(d * 64 + y2 * 4 + zp * 2 + j, 8, stride=8), :]
 
     def fill2(d, c):
         there = gy + d - 4
@@ -421,16 +467,6 @@
 
         lax.fori_loop(d0_, d1_ + 1, body, 0)
 
-    m3k, m3f = B["m3k"], B["m3f"]
-    total = jnp.zeros(T8, F32)
-    for p in range(2):
-        for zp in range(2):
-            for colour in range(2):
-                total = total + k2[colour, 9 + p, zp]
-    m3k[gy] = total * 0.125
-    for dy in line:
-        put("k3", m3k.at[gy], m3k.at[gy], 1, 0, dy)
-
     received("f1")
     d1, g1, r1, b1, p1, s1 = (B[n] for n in ("d1", "g1", "r1", "b1", "p1", "s1"))
 
@@ -461,11 +497,10 @@
             p1[q + 4, y + 8] = b1[q + 4, y + 8]
         return c
 
-    lax.fori_loop(0, 4, rest1, 0)
+    loop(0, 4, rest1)
     m2f[4, gz] = coarse2(lambda q, y: s1[q, y])
     for dz, dy in patch:
-        if abs(dy) <= 2:
-            put("f2", m2f.at[4, gz], m2f.at[4 - dy, gz], 1, dz, dy)
+        put("f2", m2f.at[4, gz], m2f.at[4 - dy, gz], 1, dz, dy)
     put1("u1", "p1", ring + far + knights)
 
     received("k3")
@@ -526,9 +561,8 @@
     m3f[gy] = total * 0.125
     for dy in line:
         put("f3", m3f.at[gy], m3f.at[gy], 1, 0, dy)
-    for dz, dy in patch:
-        if abs(dy) > 2:
-            put("f2x", m2f.at[4, gz], m2f.at[4 - dy, gz], 1, dz, dy)
+    for dy in (4, -4, 3, -3):
+        put("f2x", m2f.at[4], m2f.at[4 - dy], 8, 0, dy)
     for dy in range(-4, 5):
         if dy:
             put("u2", p2.at[pl.ds(9, 2)], p2.at[pl.ds(9 - 2 * dy, 2)], 4, 0, dy)
@@ -606,7 +640,7 @@
             e2x[z2 + 4, y2] = jnp.where((lane // 4) % 2 == 0, parts[0], parts[1])
         return c
 
-    lax.fori_loop(0, 10, spread2, 0)
+    loop(0, 10, spread2)
 
     received("u1")
     finished("u1")
@@ -618,7 +652,7 @@
                 p1[q, 2 * y2 + p] = p1[q, 2 * y2 + p] + e
         return c
 
-    lax.fori_loop(0, 10, up1, 0)
+    loop(0, 10, up1)
     half_sweep(1, 0, r1, p1, -3, 4, -6, 9)
     half_sweep(1, 1, p1, r1, -3, 4, -5, 8)
     half_sweep(1, 0, r1, p1, -2, 3, -4, 7)
@@ -662,7 +696,7 @@
             out_r[hi, :] = jnp.where(even, res_black[q], res_red[q])
         return c
 
-    lax.fori_loop(0, 8, finish, 0)
+    loop(0, 8, finish)
     for c in pieces(u_out, B["stage_f"], in_sem.at[0], True) + pieces(r_out, B["stage_k"], in_sem.at[1], True):
         c.start()
     for group in GROUPS:
@@ -692,11 +726,11 @@
         return pl.pallas_call(
             body,
             out_shape=(out, out),
-            in_specs=[pl.BlockSpec(memory_space=pl.ANY)] * 2,
+            in_specs=[pl.BlockSpec(memory_space=pltpu.HBM)] * 2,
             out_specs=[pl.BlockSpec(memory_space=pl.ANY)] * 2,
             scratch_shapes=scratch
             + [pltpu.SemaphoreType.DMA((2,)), pltpu.SemaphoreType.DMA((len(GROUPS),)), pltpu.SemaphoreType.DMA((len(GROUPS),))],
-            compiler_params=pltpu.CompilerParams(collective_id=0, has_side_effects=True, vmem_limit_bytes=56 * 1024 * 1024),
+            compiler_params=pltpu.CompilerParams(collective_id=0, has_side_effects=True, vmem_limit_bytes=40 * 1024 * 1024),
             name="vcycle",
         )(right_side, coefficient)
 

time: 83.7 us -> 69.5 us (0.83)
  Pallas kernels: 80.3 us -> 65.4 us
  local copies, waits for them, and re-layouts: 2.42 us -> 3.3 us
    pallas_call x1, Pallas kernels: 80.3 us -> 65.4 us  [on_device(): pl.pallas_call(body, out_shape=(out, out), in_specs=[pl.BlockSpec(memory_...]
    unnamed x4 -> x6, local copies, waits for them, and re-layouts: 2.42 us -> 3.3 us
where the time goes in v2:
time: 69.5 us; the launch traced here: 69.4 us
  Pallas kernels  65.4 us (94%)
  local copies, waits for them, and re-layouts  3.3 us (5%)
    pallas_call x1, Pallas kernels, on_device(): pl.pallas_call(body, out_shape=(out, out), in_specs=[pl.BlockSpec(memory_...  65.4 us
    unnamed x6, local copies, waits for them, and re-layouts  3.3 us

profile of v2, /device:TPU:1, one launch (start us, length us, event | category | flops | bytes accessed | tf_op | source)
XLA Modules:
  0.0 69.4 jit_solution(12982105719812212683)
XLA Ops:
  0.6 0.0 copy-start
  0.6 0.9 %copy-done = f32[8,8,1024]{2,1,0:T(8,128)S(1)} copy-done((f32[8,8,1024]{2,1,0:T(8,128)S(1)}, f32[8,8,1024]{2,1,0:T(8,128)}, u32[]{:S(2)}) %copy-start) | copy-done | bytes 262168
  1.6 0.0 copy-start.1
  1.6 0.9 %copy-done.1 = f32[8,8,1024]{2,1,0:T(8,128)S(1)} copy-done((f32[8,8,1024]{2,1,0:T(8,128)S(1)}, f32[8,8,1024]{2,1,0:T(8,128)}, u32[]{:S(2)}) %copy-start.1) | copy-done | bytes 262168
  2.5 65.4 %vcycle.1 = (f32[8,8,1024]{2,1,0:T(8,128)S(1)}, f32[8,8,1024]{2,1,0:T(8,128)S(1)}) custom-call(f32[8,8,1024]{2,1,0:T(8,128)S(1)} %copy-done, f32[8,8,1024]{2,1,0:T(8,128)S(1)} %copy-done.1), custom_call_target="tpu_custom_call" | custom-call | tf_op jit(solution)/shard_map/vcycle/pallas_call | solution.py:726
  68.0 0.7 %copy.6 = f32[8,8,1024]{2,1,0:T(8,128)} copy(f32[8,8,1024]{2,1,0:T(8,128)S(1)} %get-tuple-element.4) | data formatting | bytes 524288
  68.7 0.7 %copy.7 = f32[8,8,1024]{2,1,0:T(8,128)} copy(f32[8,8,1024]{2,1,0:T(8,128)S(1)} %get-tuple-element.5) | data formatting | bytes 524288
Async XLA Ops:
  0.6 1.0 %copy-start = (f32[8,8,1024]{2,1,0:T(8,128)S(1)}, f32[8,8,1024]{2,1,0:T(8,128)}, u32[]{:S(2)}) copy-start(f32[8,8,1024]{2,1,0:T(8,128)} %refs_0_.1) | copy-start | bytes 786436
  1.6 0.9 %copy-start.1 = (f32[8,8,1024]{2,1,0:T(8,128)S(1)}, f32[8,8,1024]{2,1,0:T(8,128)}, u32[]{:S(2)}) copy-start(f32[8,8,1024]{2,1,0:T(8,128)} %refs_1_.1) | copy-start | bytes 786436

commit v3 on v2

--- a/solution.py
+++ b/solution.py
@@ -14,12 +14,12 @@
     k0=(2, 10, 20), f0=(2, 8, 16), w0=(2, 6, 8, 16), d0=(2, 8, 16), g0=(2, 8, 16), r0=(10, 20), b0=(10, 20), p0=(10, 20),
     s0=(4, 8),
     c1k=(10, 20), c1f=(10, 20), k1=(2, 10, 20), w1=(2, 6, 8, 16), d1=(2, 8, 16), g1=(2, 8, 16), r1=(10, 20), b1=(10, 20), p1=(10, 20),
-    s1=(2, 4),
+    s1=(2, 4), p1c=(10, 10),
     m2k=(9, 8), m2f=(9, 8), k2=(2, 20, 2), w2=(2, 6, 18, 2), d2=(2, 18, 2), g2=(2, 18, 2), r2=(20, 2), b2=(20, 2), p2=(20, 2),
     e2v=(10, 2, 2, 3), e2x=(10, 10),
     m3k=(32,), m3f=(32,), k3=(2, 18), w3=(2, 6, 16), d3=(2, 16), g3=(2, 16), r3=(18,), b3=(18,), e3=(40,),
 )
-GROUPS = ("h0", "k1", "k2", "k2x", "f1", "f1x", "u0", "u1", "k3", "f2", "f2x", "u2", "f3")
+GROUPS = ("h0z", "h0", "k1", "k2", "k2x", "f1", "f1x", "u0", "u1", "k3", "f2", "f2x", "u2", "f3")
 
 
 def iota(dim):
@@ -57,25 +57,19 @@
     def device(dz, dy):
         return (lax.rem(gz + (dz + nz) % nz, nz), lax.rem(gy + (dy + ny) % ny, ny))
 
-    def pieces(hbm, ref, sem, out):
-        copies = []
-        for t in range(8):
-            here, there = hbm.at[:, :, pl.ds(t * 128, 128)], ref.at[:, t]
-            copies.append(pltpu.make_async_copy(there, here, sem) if out else pltpu.make_async_copy(here, there, sem))
-        return copies
-
     def wait_bytes(sem, n):
         view = B["w0"].reshape(1536, 8, 128).at[pl.ds(0, n)]
         pltpu.make_async_copy(view, view, sem).wait()
 
-    for c in pieces(k_in, B["stage_k"], in_sem.at[0], False) + pieces(f_in, B["stage_f"], in_sem.at[1], False):
-        c.start()
+    pltpu.make_async_copy(k_in, B["stage_k"], in_sem.at[0]).start()
+    pltpu.make_async_copy(f_in, B["stage_f"], in_sem.at[1]).start()
 
     ring = [(0, 1), (0, -1), (1, 1), (1, -1), (-1, 1), (-1, -1), (1, 0), (-1, 0)]
     far = [(2, 0), (-2, 0), (0, 2), (0, -2)]
     knights = [(a, b) for a in (-2, -1, 1, 2) for b in (-2, -1, 1, 2) if abs(a) != abs(b)]
+    around = ring + far + knights
+    line = sorted(range(1, ny), key=lambda b: -min(b, ny - b))
     patch = [(a, b) for b in (2, -2, 1, -1, 0) for a in range(nz) if (a, b) != (0, 0)]
-    line = sorted(range(1, ny), key=lambda b: -min(b, ny - b))
     everyone = patch + [(0, b) for b in line if 2 < b < ny - 2]
     barrier = pltpu.get_barrier_semaphore()
     for dz, dy in everyone:
@@ -135,13 +129,13 @@
         for dz, dy in ((0, 1), (0, -1)):
             for name, oq, oy, colour, depth in fields:
                 put0(group, name, oq, oy, colour, dz, dy, 0, depth)
+        for dz, dy in ((1, 0), (-1, 0)):
+            for name, oq, oy, colour, depth in fields:
+                put0(group + "z" * (group == "h0"), name, oq, oy, colour, dz, dy, (depth + 1) // 2, 0)
         for dz, dy in ((1, 1), (1, -1), (-1, 1), (-1, -1)):
             for name, oq, oy, colour, depth in fields:
                 put0(group, name, oq, oy, colour, dz, dy, 1, depth - 1)
                 put0(group, name, oq, oy, colour, dz, dy, 2, depth - 3, 1)
-        for dz, dy in ((1, 0), (-1, 0)):
-            for name, oq, oy, colour, depth in fields:
-                put0(group, name, oq, oy, colour, dz, dy, (depth + 1) // 2, 0)
 
     halo0("h0", [("k0", 3, 6, 1, 5), ("k0", 3, 6, 0, 4), ("f0", 2, 4, 0, 4), ("f0", 2, 4, 1, 3)])
 
@@ -158,17 +152,16 @@
                     B[name][index + (q, slice(y, end))] = jnp.zeros((end - y,) + T8, F32)
                 y = end + 1
 
-    def put1(group, name, which):
-        ref = B[name]
+    def put1(group, name, which, far_depth, knight_depth, rows, dry=False):
+        ref, oy = B[name], 2 * rows
         for dz, dy in which:
-            if (dz, dy) in knights:
-                sq, tq, lq = nearest(dz, 1, 2)
-                sy, ty, ly = nearest(dy, 2, 4)
+            nq, nr = (2, rows) if (dz, dy) in ring else knight_depth if (dz, dy) in knights else far_depth
+            sq, tq, lq = nearest(dz, nq, 2)
+            sy, ty, ly = nearest(dy, nr, rows)
+            if dry:
+                covered.setdefault(name, set()).update((tq + i + 4, ty + j + oy) for i in range(lq) for j in range(ly))
             else:
-                sq, tq, lq = 0, -2 * dz, 2
-                sy, ty, ly = 0, -4 * dy, 4
-            covered.setdefault((name, None), set()).update((tq + i + 4, ty + j + 8) for i in range(lq) for j in range(ly))
-            put(group, ref.at[pl.ds(sq + 4, lq), pl.ds(sy + 8, ly)], ref.at[pl.ds(tq + 4, lq), pl.ds(ty + 8, ly)], lq * ly, dz, dy)
+                put(group, ref.at[pl.ds(sq + 4, lq), pl.ds(sy + oy, ly)], ref.at[pl.ds(tq + 4, lq), pl.ds(ty + oy, ly)], lq * ly, dz, dy)
 
     def coarse1(read, target):
         def body(y1, c):
@@ -199,7 +192,7 @@
 
     k0, c1k, c1f = B["k0"], B["c1k"], B["c1f"]
     coarse1(lambda z, y: k0[0, z + 3, y + 6] + k0[1, z + 3, y + 6], c1k)
-    put1("k1", "c1k", ring + far + knights)
+    put1("k1", "c1k", around, (2, 3), (1, 2), 4)
     m2k, m2f = B["m2k"], B["m2f"]
 
     def both1(q, y):
@@ -215,8 +208,12 @@
         clear("k0", (colour,), own0, covered["k0", colour])
         clear("f0", (colour,), (2, 4, 4, 8), covered["f0", colour])
     clear("p0", (), own0, covered["k0", 1])
-    for name in ("c1k", "c1f", "p1"):
-        clear(name, (), own1, covered["c1k", None])
+    put1("", "c1k", around, (2, 3), (1, 2), 4, True)
+    put1("", "c1f", around, (1, 2), (1, 1), 4, True)
+    put1("", "p1c", around, (2, 2), (1, 1), 2, True)
+    clear("c1k", (), own1, covered["c1k"])
+    clear("c1f", (), own1, covered["c1f"])
+    clear("p1c", (), (4, 4, 2, 2), covered["p1c"])
 
     def wipe(i, c):
         for name in ("r0", "b0", "r1", "b1"):
@@ -328,29 +325,38 @@
 
     PLACE = {0: (3, 6, 2, 4, 1), 1: (4, 8, 3, 6, 2)}
 
-    received("h0")
-
     def blank(name, at):
         ref = B[name]
         shape = BUFFERS[name]
         size = [len(range(*a.indices(n))) if isinstance(a, slice) else None for a, n in zip(at, shape)]
         ref[at] = jnp.zeros(tuple(s for s in size if s is not None) + T8, F32)
 
-    ALL = slice(None)
-    for side, cut in ((gz == 0, (ALL, slice(0, 3))), (gz == nz - 1, (ALL, slice(7, 10))),
-                      (gy == 0, (ALL, ALL, slice(0, 6))), (gy == ny - 1, (ALL, ALL, slice(14, 20)))):
+    def blank0(side, qs, spans):
         @pl.when(side)
-        def _(cut=cut):
+        def _():
             for colour in range(2):
-                if len(cut) == 2:
-                    for q in range(cut[1].start, cut[1].stop):
-                        blank("k0", (colour, q, slice(0, 20)))
-                else:
-                    for q in range(10):
-                        blank("k0", (colour, q, cut[2]))
-
-    weigh(0, 0, 3, 6, 2, 4, -2, 5, -4, 11, 1)
-    weigh(0, 1, 3, 6, 2, 4, -2, 5, -3, 10, 1)
+                for q in qs:
+                    for span in spans:
+                        blank("k0", (colour, q, slice(*span)))
+
+    received("h0z")
+    blank0(gz == 0, range(0, 3), [(6, 14)])
+    blank0(gz == nz - 1, range(7, 10), [(6, 14)])
+    weigh(0, 0, 3, 6, 2, 4, -2, 5, 1, 6, 1)
+    weigh(0, 1, 3, 6, 2, 4, -2, 5, 1, 6, 1)
+    received("h0")
+    blank0(gz == 0, range(0, 3), [(0, 6), (14, 20)])
+    blank0(gz == nz - 1, range(7, 10), [(0, 6), (14, 20)])
+    blank0(gy == 0, range(10), [(0, 6)])
+    blank0(gy == ny - 1, range(10), [(14, 20)])
+    for ys in ((-1, 0), (7, 8)):
+        weigh(0, 0, 3, 6, 2, 4, -2, 5, *ys, 1)
+        weigh(0, 1, 3, 6, 2, 4, -2, 5, *ys, 1)
+    for ys in ((-3, -2), (9, 10)):
+        weigh(0, 0, 3, 6, 2, 4, -1, 4, *ys, 1)
+        weigh(0, 1, 3, 6, 2, 4, -1, 4, *ys, 1)
+    for y in (-4, 11):
+        weigh(0, 0, 3, 6, 2, 4, 0, 3, y, y, 1)
     f0, d0, g0, r0, b0, p0, s0 = (B[n] for n in ("f0", "d0", "g0", "r0", "b0", "p0", "s0"))
 
     def start0(y, c):
@@ -383,8 +389,8 @@
 
     loop(0, 8, rest0)
     coarse1(lambda z, y: s0[z, y], c1f)
-    put1("f1", "c1f", ring)
-    put1("f1x", "c1f", far + knights)
+    put1("f1", "c1f", ring, None, None, 4)
+    put1("f1x", "c1f", far + knights, (1, 2), (1, 1), 4)
     halo0("u0", [("p0", 3, 6, None, 5)])
 
     received("k1")
@@ -458,14 +464,21 @@
             acc = acc + w2[colour, i, row, zp] * u[i]
         return acc
 
-    def half_sweep2(colour, target, other, d0_, d1_):
-        def body(d, c):
-            for p in range(2):
-                for zp in range(2):
-                    target[2 * d + p + 1, zp] = fresh2(d, p, zp, colour, other)
+    def half_sweep2(colour, target, other, first, last):
+        def rows(ds):
+            at = [(d, p, zp) for d in ds for p in range(2) for zp in range(2)]
+            values = [fresh2(d, p, zp, colour, other) for d, p, zp in at]
+            for (d, p, zp), v in zip(at, values):
+                target[2 * d + p + 1, zp] = v
+
+        def body(i, c):
+            rows([3 * i + first + n for n in range(3)])
             return c
 
-        lax.fori_loop(d0_, d1_ + 1, body, 0)
+        steps = (last + 1 - first) // 3
+        lax.fori_loop(0, steps, body, 0)
+        if first + 3 * steps <= last:
+            rows(range(first + 3 * steps, last + 1))
 
     received("f1")
     d1, g1, r1, b1, p1, s1 = (B[n] for n in ("d1", "g1", "r1", "b1", "p1", "s1"))
@@ -494,14 +507,17 @@
         black = residual(1, 1, b1, r1, qs, y)
         for q in qs:
             s1[q, y] = red[q] + black[q]
-            p1[q + 4, y + 8] = b1[q + 4, y + 8]
         return c
 
     loop(0, 4, rest1)
     m2f[4, gz] = coarse2(lambda q, y: s1[q, y])
     for dz, dy in patch:
         put("f2", m2f.at[4, gz], m2f.at[4 - dy, gz], 1, dz, dy)
-    put1("u1", "p1", ring + far + knights)
+    p1c = B["p1c"]
+    for q in range(2):
+        for y in range(2):
+            p1c[q + 4, y + 4] = jnp.where(lane % 2 == 0, b1[q + 4, 2 * y + 8], pltpu.roll(b1[q + 4, 2 * y + 9], 1, 1))
+    put1("u1", "p1c", around, (2, 2), (1, 1), 2)
 
     received("k3")
     k3, w3, d3, g3, r3, b3, e3 = (B[n] for n in ("k3", "w3", "d3", "g3", "r3", "b3", "e3"))
@@ -528,7 +544,7 @@
                 w3[colour, i, m] = ws[i]
         return c
 
-    lax.fori_loop(0, 16, weigh3, 0)
+    loop(0, 16, weigh3)
 
     received("f2")
 
@@ -544,7 +560,7 @@
                             r2[row + 1, zp] = v
             return c
 
-        lax.fori_loop(d0_, d1_ + 1, body, 0)
+        loop(d0_, d1_ + 1, body)
 
     start2(2, 6, True)
     half_sweep2(1, b2, r2, 2, 6)
@@ -612,7 +628,7 @@
                 p2[2 * d + p + 1, zp] = p2[2 * d + p + 1, zp] + e
         return c
 
-    lax.fori_loop(0, 9, up2, 0)
+    loop(0, 9, up2, 3)
     half_sweep2(0, r2, p2, 0, 8)
     half_sweep2(1, p2, r2, 1, 7)
     half_sweep2(0, r2, p2, 1, 7)
@@ -628,7 +644,7 @@
                     e2v[2 * (d - 2) + p, zp, (colour + p + zp) % 2, pl.ds(8, 8), :] = ref[2 * d + p + 1, zp]
         return c
 
-    lax.fori_loop(2, 7, store2, 0)
+    loop(2, 7, store2, 5)
     spread = 16 * sub + lane // 8
 
     def spread2(y2, c):
@@ -643,13 +659,12 @@
     loop(0, 10, spread2)
 
     received("u1")
-    finished("u1")
 
     def up1(y2, c):
         for q in range(10):
             e = e2x[q, y2]
             for p in range(2):
-                p1[q, 2 * y2 + p] = p1[q, 2 * y2 + p] + e
+                p1[q, 2 * y2 + p] = (pltpu.roll(p1c[q, y2], 127, 1) if p else p1c[q, y2]) + e
         return c
 
     loop(0, 10, up1)
@@ -680,7 +695,7 @@
     half_sweep(0, 0, r0, p0, -1, 4, -2, 9)
     half_sweep(0, 1, p0, r0, -1, 4, -1, 8)
 
-    out_u, out_r = B["stage_f"].reshape(512, 128), B["stage_k"].reshape(512, 128)
+    out_u, out_r = u_out.reshape(512, 128), r_out.reshape(512, 128)
 
     def finish(y, c):
         even = (lane + y) & 1 == 0
@@ -697,20 +712,23 @@
         return c
 
     loop(0, 8, finish)
-    for c in pieces(u_out, B["stage_f"], in_sem.at[0], True) + pieces(r_out, B["stage_k"], in_sem.at[1], True):
-        c.start()
     for group in GROUPS:
-        if group not in ("u0", "u1", "u2"):
+        if group not in ("u0", "u2"):
             finished(group)
-    wait_bytes(in_sem.at[0], 64)
-    wait_bytes(in_sem.at[1], 64)
 
 
 def solution(mesh):
     nz, ny = mesh.shape["gz"], mesh.shape["gy"]
 
     def on_device(right_side, coefficient):
-        out = jax.ShapeDtypeStruct(right_side.shape, F32)
+        depth, rows, width = right_side.shape
+        out = jax.ShapeDtypeStruct((depth, width // 128, rows, 128), F32)
+
+        def tiles(array):
+            return array.reshape(depth, rows, width // 128, 128).transpose(0, 2, 1, 3)
+
+        def whole(array):
+            return array.transpose(0, 2, 1, 3).reshape(depth, rows, width)
 
         def body(*refs):
             kernel(nz, ny, *refs)
@@ -723,16 +741,17 @@
                 scratch.append(pltpu.VMEM((10, 2, 2, 24, 128), F32))
             else:
                 scratch.append(pltpu.VMEM(shape + T8, F32))
-        return pl.pallas_call(
+        correction, residual = pl.pallas_call(
             body,
             out_shape=(out, out),
             in_specs=[pl.BlockSpec(memory_space=pltpu.HBM)] * 2,
-            out_specs=[pl.BlockSpec(memory_space=pl.ANY)] * 2,
+            out_specs=[pl.BlockSpec(memory_space=pltpu.VMEM)] * 2,
             scratch_shapes=scratch
             + [pltpu.SemaphoreType.DMA((2,)), pltpu.SemaphoreType.DMA((len(GROUPS),)), pltpu.SemaphoreType.DMA((len(GROUPS),))],
             compiler_params=pltpu.CompilerParams(collective_id=0, has_side_effects=True, vmem_limit_bytes=40 * 1024 * 1024),
             name="vcycle",
-        )(right_side, coefficient)
+        )(tiles(right_side), tiles(coefficient))
+        return whole(correction), whole(residual)
 
     placed = (P("gz", "gy", None), P("gz", "gy", None))
     return jax.shard_map(on_device, mesh=mesh, in_specs=placed, out_specs=placed, check_vma=False)

time: 69.5 us -> 66.1 us (0.951)
  Pallas kernels: 65.4 us -> 62 us
    pallas_call x1, Pallas kernels: 65.4 us -> 62 us  [on_device(): pl.pallas_call(body, out_shape=(out, out), in_specs=[pl.BlockSpec(memory_...]
where the time goes in v3:
time: 66.1 us; the launch traced here: 65.9 us
  Pallas kernels  62 us (94%)
  local copies, waits for them, and re-layouts  3.3 us (5%)
    pallas_call x1, Pallas kernels, on_device(): pl.pallas_call(body, out_shape=(out, out), in_specs=[pl.BlockSpec(memory_...  62 us
    unnamed x6, local copies, waits for them, and re-layouts  3.3 us

profile of v3, /device:TPU:1, one launch (start us, length us, event | category | flops | bytes accessed | tf_op | source)
XLA Modules:
  0.0 65.9 jit_solution(1518658832272475203)
XLA Ops:
  0.6 0.0 copy-start
  0.6 0.9 %copy-done = f32[8,8,1024]{2,1,0:T(8,128)S(1)} copy-done((f32[8,8,1024]{2,1,0:T(8,128)S(1)}, f32[8,8,1024]{2,1,0:T(8,128)}, u32[]{:S(2)}) %copy-start) | copy-done | bytes 262168
  1.6 0.0 copy-start.1
  1.6 0.9 %copy-done.1 = f32[8,8,1024]{2,1,0:T(8,128)S(1)} copy-done((f32[8,8,1024]{2,1,0:T(8,128)S(1)}, f32[8,8,1024]{2,1,0:T(8,128)}, u32[]{:S(2)}) %copy-start.1) | copy-done | bytes 262168
  2.5 62.0 %vcycle.1 = (f32[8,8,8,128]{3,2,1,0:T(8,128)S(1)}, f32[8,8,8,128]{3,2,1,0:T(8,128)S(1)}) custom-call(f32[8,8,8,128]{3,2,1,0:T(8,128)S(1)} %bitcast.12, f32[8,8,8,128]{3,2,1,0:T(8,128)S(1)} %bitcast.13), custom_call_target="tpu_custom_call" | custom-call | tf_op jit(solution)/shard_map/vcycle/pallas_call | solution.py:744
  64.5 0.7 %copy.6 = f32[8,8,1024]{2,1,0:T(8,128)} copy(f32[8,8,1024]{2,1,0:T(8,128)S(1)} %bitcast.15) | data formatting | bytes 524288
  65.2 0.7 %copy.7 = f32[8,8,1024]{2,1,0:T(8,128)} copy(f32[8,8,1024]{2,1,0:T(8,128)S(1)} %bitcast.14) | data formatting | bytes 524288
Async XLA Ops:
  0.6 1.0 %copy-start = (f32[8,8,1024]{2,1,0:T(8,128)S(1)}, f32[8,8,1024]{2,1,0:T(8,128)}, u32[]{:S(2)}) copy-start(f32[8,8,1024]{2,1,0:T(8,128)} %param.2) | copy-start | bytes 786436
  1.6 0.9 %copy-start.1 = (f32[8,8,1024]{2,1,0:T(8,128)S(1)}, f32[8,8,1024]{2,1,0:T(8,128)}, u32[]{:S(2)}) copy-start(f32[8,8,1024]{2,1,0:T(8,128)} %param.3) | copy-start | bytes 786436

commit v4 on v3

--- a/solution.py
+++ b/solution.py
@@ -192,7 +192,6 @@
 
     k0, c1k, c1f = B["k0"], B["c1k"], B["c1f"]
     coarse1(lambda z, y: k0[0, z + 3, y + 6] + k0[1, z + 3, y + 6], c1k)
-    put1("k1", "c1k", around, (2, 3), (1, 2), 4)
     m2k, m2f = B["m2k"], B["m2f"]
 
     def both1(q, y):
@@ -239,17 +238,6 @@
     def open2(ref, d, y2, zp, j):
         return ref.reshape(576, 128)[pl.ds(d * 64 + y2 * 4 + zp * 2 + j, 8, stride=8), :]
 
-    received("k2")
-    total = jnp.zeros(T8, F32)
-    for n in range(8):
-        total = total + open2(m2k, 4, n // 4, n // 2 % 2, n % 2)
-    m3k, m3f = B["m3k"], B["m3f"]
-    m3k[gy] = total * 0.125
-    for dy in (4, -4, 3, -3, 2, -2, 1, -1):
-        put("k2x", m2k.at[4], m2k.at[4 - dy], 8, 0, dy)
-    for dy in line:
-        put("k3", m3k.at[gy], m3k.at[gy], 1, 0, dy)
-
     def shifts(v, st, edge):
         a = pltpu.roll(v, st, 1)
         m = jnp.where(lane < st, pltpu.roll(a, 1, 0), a)
@@ -307,15 +295,20 @@
 
         qs = list(range(q0, q1 + 1))
 
-        def body(i, c):
-            rows = [2 * i + y0, 2 * i + y0 + 1]
-            values = [fresh(level, colour, qs, y, other, oq, oy, wq, wy, st) for y in rows]
-            for y, row in zip(rows, values):
+        def rows(ys):
+            values = [fresh(level, colour, qs, y, other, oq, oy, wq, wy, st) for y in ys]
+            for y, row in zip(ys, values):
                 for q, v in zip(qs, row):
                     target[q + oq, y + oy] = v
+
+        def body(i, c):
+            rows([4 * i + y0 + n for n in range(4)])
             return c
 
-        lax.fori_loop(0, (y1 + 1 - y0) // 2, body, 0)
+        steps = (y1 + 1 - y0) // 4
+        lax.fori_loop(0, steps, body, 0)
+        if y0 + 4 * steps <= y1:
+            rows(range(y0 + 4 * steps, y1 + 1))
 
     def residual(level, colour, own, other, qs, y):
         oq, oy, wq, wy, st = PLACE[level]
@@ -339,11 +332,29 @@
                     for span in spans:
                         blank("k0", (colour, q, slice(*span)))
 
+    f0, d0, g0, r0, b0, p0, s0 = (B[n] for n in ("f0", "d0", "g0", "r0", "b0", "p0", "s0"))
+
+    def start0(y, c):
+        for q in range(8):
+            red = f0[0, q, y] * d0[0, q, y]
+            g0[0, q, y] = red
+            r0[q + 1, y + 2] = red
+        return c
+
+
+    def start0b(y, c):
+        for q in range(8):
+            g0[1, q, y] = f0[1, q, y] * d0[1, q, y]
+        return c
+
     received("h0z")
     blank0(gz == 0, range(0, 3), [(6, 14)])
     blank0(gz == nz - 1, range(7, 10), [(6, 14)])
     weigh(0, 0, 3, 6, 2, 4, -2, 5, 1, 6, 1)
     weigh(0, 1, 3, 6, 2, 4, -2, 5, 1, 6, 1)
+    loop(5, 11, start0)
+    loop(5, 11, start0b)
+    put1("k1", "c1k", around, (2, 3), (1, 2), 4)
     received("h0")
     blank0(gz == 0, range(0, 3), [(0, 6), (14, 20)])
     blank0(gz == nz - 1, range(7, 10), [(0, 6), (14, 20)])
@@ -357,23 +368,10 @@
         weigh(0, 1, 3, 6, 2, 4, -1, 4, *ys, 1)
     for y in (-4, 11):
         weigh(0, 0, 3, 6, 2, 4, 0, 3, y, y, 1)
-    f0, d0, g0, r0, b0, p0, s0 = (B[n] for n in ("f0", "d0", "g0", "r0", "b0", "p0", "s0"))
-
-    def start0(y, c):
-        for q in range(8):
-            red = f0[0, q, y] * d0[0, q, y]
-            g0[0, q, y] = red
-            r0[q + 1, y + 2] = red
-        return c
-
-    loop(0, 16, start0)
-
-    def start0b(y, c):
-        for q in range(8):
-            g0[1, q, y] = f0[1, q, y] * d0[1, q, y]
-        return c
-
-    loop(1, 15, start0b)
+    loop(0, 5, start0)
+    loop(11, 16, start0)
+    loop(1, 5, start0b)
+    loop(11, 15, start0b)
     half_sweep(0, 1, b0, r0, -2, 5, -3, 10)
     half_sweep(0, 0, r0, b0, -1, 4, -2, 9)
     half_sweep(0, 1, b0, r0, -1, 4, -1, 8)
@@ -390,8 +388,16 @@
     loop(0, 8, rest0)
     coarse1(lambda z, y: s0[z, y], c1f)
     put1("f1", "c1f", ring, None, None, 4)
-    put1("f1x", "c1f", far + knights, (1, 2), (1, 1), 4)
-    halo0("u0", [("p0", 3, 6, None, 5)])
+    received("k2")
+    total = jnp.zeros(T8, F32)
+    for n in range(8):
+        total = total + open2(m2k, 4, n // 4, n // 2 % 2, n % 2)
+    m3k, m3f = B["m3k"], B["m3f"]
+    m3k[gy] = total * 0.125
+    for dy in (4, -4, 3, -3, 2, -2, 1, -1):
+        put("k2x", m2k.at[4], m2k.at[4 - dy], 8, 0, dy)
+    for dy in line:
+        put("k3", m3k.at[gy], m3k.at[gy], 1, 0, dy)
 
     received("k1")
     k1 = B["k1"]
@@ -413,7 +419,6 @@
     weigh(1, 0, 4, 8, 3, 6, -3, 4, -6, 9, 2)
     weigh(1, 1, 4, 8, 3, 6, -3, 4, -5, 8, 2)
 
-    received("k2x")
     k2, w2, d2, g2, r2, b2, p2 = (B[n] for n in ("k2", "w2", "d2", "g2", "r2", "b2", "p2"))
 
     def fill2(d, c):
@@ -425,7 +430,6 @@
                     k2[colour, 2 * d + y2 + 1, zp] = open2(m2k, d, y2, zp, (colour + y2 + zp) % 2) * inside
         return c
 
-    lax.fori_loop(0, 9, fill2, 0)
 
     def near2(ref, row, p, zp, colour, edge):
         o, oz = ref[row, zp], ref[row, 1 - zp]
@@ -454,7 +458,6 @@
                         w2[colour, i, row, zp] = ws[i]
         return c
 
-    lax.fori_loop(0, 9, weigh2, 0)
 
     def fresh2(d, p, zp, colour, other):
         row = 2 * d + p
@@ -513,11 +516,15 @@
     m2f[4, gz] = coarse2(lambda q, y: s1[q, y])
     for dz, dy in patch:
         put("f2", m2f.at[4, gz], m2f.at[4 - dy, gz], 1, dz, dy)
+    put1("f1x", "c1f", far + knights, (1, 2), (1, 1), 4)
     p1c = B["p1c"]
     for q in range(2):
         for y in range(2):
             p1c[q + 4, y + 4] = jnp.where(lane % 2 == 0, b1[q + 4, 2 * y + 8], pltpu.roll(b1[q + 4, 2 * y + 9], 1, 1))
     put1("u1", "p1c", around, (2, 2), (1, 1), 2)
+    received("k2x")
+    loop(0, 9, fill2, 3)
+    loop(0, 9, weigh2)
 
     received("k3")
     k3, w3, d3, g3, r3, b3, e3 = (B[n] for n in ("k3", "w3", "d3", "g3", "r3", "b3", "e3"))
@@ -583,6 +590,8 @@
         if dy:
             put("u2", p2.at[pl.ds(9, 2)], p2.at[pl.ds(9 - 2 * dy, 2)], 4, 0, dy)
 
+    halo0("u0", [("p0", 3, 6, None, 5)])
+
     received("f1x")
     start1(-3, 4, -6, 9, False)
 

time: 66.1 us -> 61.8 us (0.935)
  Pallas kernels: 62 us -> 57.7 us
    pallas_call x1, Pallas kernels: 62 us -> 57.7 us  [on_device(): pl.pallas_call(body, out_shape=(out, out), in_specs=[pl.BlockSpec(memory_...]
where the time goes in v4:
time: 61.8 us; the launch traced here: 61.7 us
  Pallas kernels  57.7 us (93%)
  local copies, waits for them, and re-layouts  3.3 us (5%)
  between operations  0.65 us (1%)
    pallas_call x1, Pallas kernels, on_device(): pl.pallas_call(body, out_shape=(out, out), in_specs=[pl.BlockSpec(memory_...  57.7 us
    unnamed x6, local copies, waits for them, and re-layouts  3.3 us

profile of v4, /device:TPU:1, one launch (start us, length us, event | category | flops | bytes accessed | tf_op | source)
XLA Modules:
  0.0 61.7 jit_solution(12676216055482161536)
XLA Ops:
  0.6 0.0 copy-start
  0.6 0.9 %copy-done = f32[8,8,1024]{2,1,0:T(8,128)S(1)} copy-done((f32[8,8,1024]{2,1,0:T(8,128)S(1)}, f32[8,8,1024]{2,1,0:T(8,128)}, u32[]{:S(2)}) %copy-start) | copy-done | bytes 262168
  1.6 0.0 copy-start.1
  1.6 0.9 %copy-done.1 = f32[8,8,1024]{2,1,0:T(8,128)S(1)} copy-done((f32[8,8,1024]{2,1,0:T(8,128)S(1)}, f32[8,8,1024]{2,1,0:T(8,128)}, u32[]{:S(2)}) %copy-start.1) | copy-done | bytes 262168
  2.5 57.7 %vcycle.1 = (f32[8,8,8,128]{3,2,1,0:T(8,128)S(1)}, f32[8,8,8,128]{3,2,1,0:T(8,128)S(1)}) custom-call(f32[8,8,8,128]{3,2,1,0:T(8,128)S(1)} %bitcast.12, f32[8,8,8,128]{3,2,1,0:T(8,128)S(1)} %bitcast.13), custom_call_target="tpu_custom_call" | custom-call | tf_op jit(solution)/shard_map/vcycle/pallas_call | solution.py:753
  60.2 0.7 %copy.6 = f32[8,8,1024]{2,1,0:T(8,128)} copy(f32[8,8,1024]{2,1,0:T(8,128)S(1)} %bitcast.15) | data formatting | bytes 524288
  61.0 0.7 %copy.7 = f32[8,8,1024]{2,1,0:T(8,128)} copy(f32[8,8,1024]{2,1,0:T(8,128)S(1)} %bitcast.14) | data formatting | bytes 524288
Async XLA Ops:
  0.6 1.0 %copy-start = (f32[8,8,1024]{2,1,0:T(8,128)S(1)}, f32[8,8,1024]{2,1,0:T(8,128)}, u32[]{:S(2)}) copy-start(f32[8,8,1024]{2,1,0:T(8,128)} %param.2) | copy-start | bytes 786436
  1.6 0.9 %copy-start.1 = (f32[8,8,1024]{2,1,0:T(8,128)S(1)}, f32[8,8,1024]{2,1,0:T(8,128)}, u32[]{:S(2)}) copy-start(f32[8,8,1024]{2,1,0:T(8,128)} %param.3) | copy-start | bytes 786436

commit v5 on v4

--- a/solution.py
+++ b/solution.py
@@ -102,7 +102,7 @@
                 target[1, q + oq, y + oy] = jnp.where(even, hi, lo)
             return c
 
-        loop(0, 8, body)
+        loop(0, 8, body, 4)
 
     wait_bytes(in_sem.at[0], 64)
     packed("stage_k", "k0", 3, 6)
@@ -176,7 +176,7 @@
                 target[q + 4, y1 + 8] = jnp.where(lane % 2 == 0, red, pltpu.roll(black, 1, 1))
             return c
 
-        loop(0, 4, body)
+        loop(0, 4, body, 4)
 
     def coarse2(read):
         out = jnp.zeros(T8, F32)
@@ -385,7 +385,7 @@
             p0[q + 3, y + 6] = b0[q + 3, y + 6]
         return c
 
-    loop(0, 8, rest0)
+    loop(0, 8, rest0, 4)
     coarse1(lambda z, y: s0[z, y], c1f)
     put1("f1", "c1f", ring, None, None, 4)
     received("k2")
@@ -475,13 +475,13 @@
                 target[2 * d + p + 1, zp] = v
 
         def body(i, c):
-            rows([3 * i + first + n for n in range(3)])
+            rows([4 * i + first + n for n in range(4)])
             return c
 
-        steps = (last + 1 - first) // 3
+        steps = (last + 1 - first) // 4
         lax.fori_loop(0, steps, body, 0)
-        if first + 3 * steps <= last:
-            rows(range(first + 3 * steps, last + 1))
+        if first + 4 * steps <= last:
+            rows(range(first + 4 * steps, last + 1))
 
     received("f1")
     d1, g1, r1, b1, p1, s1 = (B[n] for n in ("d1", "g1", "r1", "b1", "p1", "s1"))
@@ -512,7 +512,7 @@
             s1[q, y] = red[q] + black[q]
         return c
 
-    loop(0, 4, rest1)
+    loop(0, 4, rest1, 4)
     m2f[4, gz] = coarse2(lambda q, y: s1[q, y])
     for dz, dy in patch:
         put("f2", m2f.at[4, gz], m2f.at[4 - dy, gz], 1, dz, dy)
@@ -665,7 +665,7 @@
             e2x[z2 + 4, y2] = jnp.where((lane // 4) % 2 == 0, parts[0], parts[1])
         return c
 
-    loop(0, 10, spread2)
+    loop(0, 10, spread2, 5)
 
     received("u1")
 
@@ -676,7 +676,7 @@
                 p1[q, 2 * y2 + p] = (pltpu.roll(p1c[q, y2], 127, 1) if p else p1c[q, y2]) + e
         return c
 
-    loop(0, 10, up1)
+    loop(0, 10, up1, 5)
     half_sweep(1, 0, r1, p1, -3, 4, -6, 9)
     half_sweep(1, 1, p1, r1, -3, 4, -5, 8)
     half_sweep(1, 0, r1, p1, -2, 3, -4, 7)
@@ -698,7 +698,7 @@
                         p0[z1 + 3, 2 * y1 + i + 6] = p0[z1 + 3, 2 * y1 + i + 6] + e
         return c
 
-    loop(-3, 7, up0)
+    loop(-3, 7, up0, 5)
     half_sweep(0, 0, r0, p0, -2, 5, -4, 11)
     half_sweep(0, 1, p0, r0, -2, 5, -3, 10)
     half_sweep(0, 0, r0, p0, -1, 4, -2, 9)
@@ -720,7 +720,7 @@
             out_r[hi, :] = jnp.where(even, res_black[q], res_red[q])
         return c
 
-    loop(0, 8, finish)
+    loop(0, 8, finish, 4)
     for group in GROUPS:
         if group not in ("u0", "u2"):
             finished(group)

time: 61.8 us -> 61.1 us (0.989)
  Pallas kernels: 57.7 us -> 57 us
    pallas_call x1, Pallas kernels: 57.7 us -> 57 us  [on_device(): pl.pallas_call(body, out_shape=(out, out), in_specs=[pl.BlockSpec(memory_...]
where the time goes in v5:
time: 61.1 us; the launch traced here: 60.9 us
  Pallas kernels  57 us (93%)
  local copies, waits for them, and re-layouts  3.3 us (5%)
  between operations  0.65 us (1%)
    pallas_call x1, Pallas kernels, on_device(): pl.pallas_call(body, out_shape=(out, out), in_specs=[pl.BlockSpec(memory_...  57 us
    unnamed x6, local copies, waits for them, and re-layouts  3.3 us

profile of v5, /device:TPU:1, one launch (start us, length us, event | category | flops | bytes accessed | tf_op | source)
XLA Modules:
  0.0 60.9 jit_solution(9334163987097300470)
XLA Ops:
  0.6 0.0 copy-start
  0.6 0.9 %copy-done = f32[8,8,1024]{2,1,0:T(8,128)S(1)} copy-done((f32[8,8,1024]{2,1,0:T(8,128)S(1)}, f32[8,8,1024]{2,1,0:T(8,128)}, u32[]{:S(2)}) %copy-start) | copy-done | bytes 262168
  1.6 0.0 copy-start.1
  1.6 0.9 %copy-done.1 = f32[8,8,1024]{2,1,0:T(8,128)S(1)} copy-done((f32[8,8,1024]{2,1,0:T(8,128)S(1)}, f32[8,8,1024]{2,1,0:T(8,128)}, u32[]{:S(2)}) %copy-start.1) | copy-done | bytes 262168
  2.5 57.0 %vcycle.1 = (f32[8,8,8,128]{3,2,1,0:T(8,128)S(1)}, f32[8,8,8,128]{3,2,1,0:T(8,128)S(1)}) custom-call(f32[8,8,8,128]{3,2,1,0:T(8,128)S(1)} %bitcast.12, f32[8,8,8,128]{3,2,1,0:T(8,128)S(1)} %bitcast.13), custom_call_target="tpu_custom_call" | custom-call | tf_op jit(solution)/shard_map/vcycle/pallas_call | solution.py:753
  59.5 0.7 %copy.6 = f32[8,8,1024]{2,1,0:T(8,128)} copy(f32[8,8,1024]{2,1,0:T(8,128)S(1)} %bitcast.15) | data formatting | bytes 524288
  60.2 0.7 %copy.7 = f32[8,8,1024]{2,1,0:T(8,128)} copy(f32[8,8,1024]{2,1,0:T(8,128)S(1)} %bitcast.14) | data formatting | bytes 524288
Async XLA Ops:
  0.6 1.0 %copy-start = (f32[8,8,1024]{2,1,0:T(8,128)S(1)}, f32[8,8,1024]{2,1,0:T(8,128)}, u32[]{:S(2)}) copy-start(f32[8,8,1024]{2,1,0:T(8,128)} %param.2) | copy-start | bytes 786436
  1.6 0.9 %copy-start.1 = (f32[8,8,1024]{2,1,0:T(8,128)S(1)}, f32[8,8,1024]{2,1,0:T(8,128)}, u32[]{:S(2)}) copy-start(f32[8,8,1024]{2,1,0:T(8,128)} %param.3) | copy-start | bytes 786436
